TPU v7x, 512 devices: a whole 4x4x16 slice. The times are simulated.
512 devices in a mesh: dp: 32 (over x, z_hi, core), seq: 16 (over y, z_lo).
Axes of the slice: x: 4, y: 4, z: 16 (z_hi: 4, z_lo: 4; z = z_hi * 4 + z_lo), core: 2. Of those that a mesh axis runs over, the one named last changes fastest.
Arguments:
- saved_acts: bfloat16 [196608, 3072], P(('dp', 'seq')), may hold values from -60 to 60
- out_grads: bfloat16 [196608, 1536], P(('dp', 'seq')), may hold values from -60 to 60
- master_weight: float32 [3072, 1536], P('seq', 'dp'), may hold values from -0.109375 to 0.109375
- first_moment: float32 [3072, 1536], P('seq', 'dp'), may hold values from -2 to 2
- second_moment: float32 [3072, 1536], P('seq', 'dp'), may hold values from 0.01 to 1
Outputs:
- new_master: float32 [3072, 1536], P('seq', 'dp')
- new_first: float32 [3072, 1536], P('seq', 'dp')
- new_second: float32 [3072, 1536], P('seq', 'dp')
- new_params: bfloat16 [3072, 1536], P('seq')
All inputs are finite; a program needn't handle non-finite values.
Results may differ from a plain program's by a relative error of at most 0.0018.
Values may be sent and summed in bfloat16 or wider, within the bound.
No kernel may reach another device: no remote copies, remote signals or barrier semaphores. Data moves between devices by JAX's collectives and lax.ppermute only.
A program may use at most 64 MiB of HBM per device.

v0:
```python
import jax
import jax.numpy as jnp
from jax import lax
from jax.sharding import PartitionSpec as P

D = 3072
FO = 1536


def local(saved_acts, out_grads, master_weight, first_moment, second_moment):
    out_width = out_grads.shape[1]
    local_term = lax.dot_general(
        saved_acts, out_grads, (((0,), (0,)), ((), ())), preferred_element_type=jnp.float32
    ).astype(jnp.bfloat16)
    received = lax.all_to_all(local_term, "seq", split_axis=0, concat_axis=0, tiled=True)
    seq_count = lax.axis_size("seq")
    received = received.reshape(seq_count, received.shape[0] // seq_count, out_width)
    row_sum = jnp.sum(received, axis=0, dtype=jnp.float32)
    grad_shard = lax.psum_scatter(row_sum, "dp", scatter_dimension=1, tiled=True)
    total_sq = lax.psum(jnp.sum(grad_shard * grad_shard), ("dp", "seq"))
    rms = jnp.sqrt(total_sq / (D * FO) + 1e-06)
    clip = jnp.minimum(1.0, 1.0 / rms)
    clipped = clip * grad_shard
    new_first = 0.9 * first_moment + 0.1 * clipped
    new_second = 0.95 * second_moment + 0.05 * clipped * clipped
    new_master = master_weight - 0.01 * (
        new_first / (jnp.sqrt(new_second) + 1e-08) + 0.1 * master_weight
    )
    new_params = lax.all_gather(new_master.astype(jnp.bfloat16), "dp", axis=1, tiled=True)
    return (new_master, new_first, new_second, new_params)


def solution(mesh):
    return jax.shard_map(
        local,
        mesh=mesh,
        in_specs=(
            P(("dp", "seq"), None),
            P(("dp", "seq"), None),
            P("seq", "dp"),
            P("seq", "dp"),
            P("seq", "dp"),
        ),
        out_specs=(P("seq", "dp"), P("seq", "dp"), P("seq", "dp"), P("seq", None)),
        check_vma=False,
    )
```

profile of v0, /device:TPU:1, one launch (start us, length us, event | category | flops | bytes accessed | tf_op | source)
XLA Modules:
  0.0 518.3 jit_solution(11150093862533663829)
XLA Ops:
  7.2 0.0 copy-start
  7.2 0.0 reduce-scatter.4.cloned.1.call-start
  7.2 1.6 copy-done
  8.8 6.6 %convolution_convert_fusion = bf16[3072,1536]{1,0:T(8,128)(2,1)S(1)} fusion(bf16[384,3072]{1,0:T(8,128)(2,1)S(1)} %copy-done, bf16[384,1536]{1,0:T(8,128)(2,1)} %param.6), kind=kOutput, calls=%fused_computation.1 | convolution fusion | flops 3628597248 | bytes 12976128 | tf_op jit(solution)/shard_map/dot_general | solution.py:12
  15.4 215.7 %all_to_all.9 = bf16[16,192,1536]{2,1,0:T(8,128)(2,1)S(1)} all-to-all(bf16[16,192,1536]{2,1,0:T(8,128)(2,1)S(1)} %bitcast.9), channel_id=1, replica_groups=mesh['dp'=32,'seq'=16] {'seq'}, dimensions={0} | all-to-all | bytes 18874368 | tf_op jit(solution)/shard_map/all_to_all | solution.py:15
  231.1 1.3 convert_reduce_fusion
  232.5 1.6 copy.30
  234.1 0.0 reduce-scatter.4.cloned.1.call-update
  234.1 116.6 %reduce-scatter.4.cloned.1.call-done = f32[48,192]{1,0:T(8,128)} async-done(((f32[1536,192]{1,0:T(8,128)}), f32[48,192]{1,0:T(8,128)}) %reduce-scatter.4.cloned.1.call-update) | async-done | bytes 36880
  350.7 0.9 copy.31
  351.6 0.6 multiply_reduce_fusion
  352.2 101.6 %psum.7 = f32[]{:T(128)} all-reduce(f32[]{:T(128)} %multiply_reduce_fusion), channel_id=1, replica_groups=mesh['dp'=32,'seq'=16] {'dp','seq'}, use_global_device_ids=true, to_apply=%region_3.0 | all-reduce | flops 1 | bytes 8 | tf_op jit(solution)/shard_map/psum | solution.py:20
  454.5 1.5 fusion.1
  456.0 54.3 %all_gather.3 = bf16[192,1536]{0,1:T(8,128)(2,1)S(1)} all-gather(bf16[192,48]{0,1:T(8,128)(2,1)S(1)} %get-tuple-element.16), channel_id=1, replica_groups=mesh['dp'=32,'seq'=16] {'dp'}, dimensions={1}, use_global_device_ids=true | all-gather | bytes 608256 | tf_op jit(solution)/shard_map/all_gather | solution.py:29
  510.4 1.1 copy.29
Async XLA Ops:
  7.2 1.7 copy-start
  7.2 343.5 %reduce-scatter.4.cloned.1.call-start = ((), (), s32[]{:S(2)}) async-start(), calls=%async_computation.2 | async-start | bytes 1622016
Sparse Core Ops, SparseCore 0:
  234.2 116.4 reduce-scatter.3
where the time goes:
time: 519 us; the launch traced here: 518 us
  blocking collectives  372 us (72%)
  waiting for transfers between devices  117 us (23%)
  between operations  14.7 us (3%)
  matrix products  6.6 us (1%)
  local copies, waits for them, and re-layouts  5.21 us (1%)
    all_to_all x1, blocking collectives, local(): lax.all_to_all(local_term, 'seq', split_axis=0, concat_axis=0, tiled=True)  216 us
    unnamed x2, waiting for transfers between devices  117 us
    psum x1, blocking collectives, local(): total_sq = lax.psum(jnp.sum(grad_shard * grad_shard), ('dp', 'seq'))  102 us
    all_gather x1, blocking collectives, local(): lax.all_gather(new_master.astype(jnp.bfloat16), 'dp', axis=1, tiled=True)  54.3 us
  transfers between devices with their start and end apart: 1, of which 1 were waited for; matrix products, arithmetic and copies ran while one was open for 0% of the time, Pallas kernels for 0%

commit v1 on v0

v1 whole, which is shorter than its diff:
```python
import jax
import jax.numpy as jnp
from jax import lax
from jax.experimental import pallas as pl
from jax.experimental.pallas import tpu as pltpu
from jax.sharding import Mesh, PartitionSpec as P

D = 3072
FO = 1536
TOK = 384
F32 = jnp.float32
F16 = jnp.float16
BF16 = jnp.bfloat16


def swap(value, axis):
    return lax.ppermute(value, axis, [(0, 1), (1, 0)])


def shift(value, axis, step):
    return lax.ppermute(value, axis, [(i, (i + step) % 4) for i in range(4)])


def trade(value, axes):
    return lax.all_to_all(value, axes, 0, 0, tiled=True)


def spread(scalar, axes, count):
    return trade(jnp.broadcast_to(scalar, (count, 8, 128)), axes)[:, 0, 0]


def pick(value, index):
    return lax.dynamic_index_in_dim(value, index, 0, keepdims=False)


def eighth(value):
    value = value * value
    value = value * value
    return value * value


def arrange_kernel(core_ref, grads_ref, acts_ref, mine_ref, other_ref):
    def write(even_ref, odd_ref):
        for x in range(4):
            block = grads_ref[:, x * 384:(x + 1) * 384].T
            for zh in range(4):
                to = (zh // 2) * 384 + x * 96 + (zh % 2) * 48
                even_ref[to:to + 48, :] = block[zh * 96:zh * 96 + 48]
                odd_ref[to:to + 48, :] = block[zh * 96 + 48:zh * 96 + 96]

    @pl.when(core_ref[0] == 0)
    def _():
        write(mine_ref, other_ref)

    @pl.when(core_ref[0] != 0)
    def _():
        write(other_ref, mine_ref)

    def peak(ref):
        top = jnp.abs(ref[0:16, :])
        for row in range(16, TOK, 16):
            top = jnp.maximum(top, jnp.abs(ref[row:row + 16, :]))
        return jnp.max(top.astype(F32))

    acts_peak, grads_peak = peak(acts_ref), peak(grads_ref)
    for ref in (mine_ref, other_ref):
        ref[768:784, 0:128] = jnp.full((16, 128), acts_peak, F32).astype(BF16)
        ref[768:784, 128:384] = jnp.full((16, 256), grads_peak, F32).astype(BF16)


def arrange(core, grads, acts):
    vmem = pl.BlockSpec(memory_space=pltpu.VMEM)
    return pl.pallas_call(
        arrange_kernel,
        out_shape=[jax.ShapeDtypeStruct((784, TOK), BF16)] * 2,
        in_specs=[pl.BlockSpec(memory_space=pltpu.SMEM), vmem, vmem],
        out_specs=[vmem, vmem],
        compiler_params=pltpu.CompilerParams(vmem_limit_bytes=24 << 20),
    )(core.reshape(1), grads, acts)


def own_kernel(cols_ref, acts_ref, out_ref):
    for half in range(2):
        rows = slice(384 * half, 384 * (half + 1))
        out_ref[rows, :] = jnp.dot(cols_ref[rows, :], acts_ref[...], preferred_element_type=F32).astype(BF16)


def own_terms(cols, acts):
    return pl.pallas_call(
        own_kernel,
        grid=(4,),
        out_shape=jax.ShapeDtypeStruct((768, D), BF16),
        in_specs=[pl.BlockSpec((784, TOK), lambda i: (0, 0)), pl.BlockSpec((TOK, 768), lambda i: (0, i))],
        out_specs=pl.BlockSpec((768, 768), lambda i: (0, i)),
        compiler_params=pltpu.CompilerParams(vmem_limit_bytes=32 << 20),
        cost_estimate=pl.CostEstimate(flops=2 * 768 * TOK * D, bytes_accessed=8 << 20, transcendentals=0),
    )(cols, acts)


def pair_kernel(mine_ref, their_ref, acts_ref, own_ref, over_x_ref, over_y_ref):
    step = pl.program_id(0)
    bound = jnp.zeros((16, 128), F32)
    for ref in (mine_ref, their_ref):
        bound = bound + TOK * ref[768:784, 0:128].astype(F32) * ref[768:784, 128:256].astype(F32)
    up = jnp.full((16, 128), 2.0 ** -14, F32)
    down = jnp.full((16, 128), 2.0 ** 14, F32)
    for k in range(-14, 14):
        over = bound > 2.0 ** (8 * k)
        up = jnp.where(over, up * 2.0, up)
        down = jnp.where(over, down * 0.5, down)
    scale = eighth(down[0:1, 0:1]) * 2.0 ** 15
    up = jnp.broadcast_to(up[0:1, 0:1], (8, 768))
    down = jnp.broadcast_to(down[0:1, 0:1], (8, 768))

    for half in range(2):
        rows = slice(384 * half, 384 * (half + 1))
        term = jnp.dot(their_ref[rows, :], acts_ref[...], preferred_element_type=F32).astype(BF16)
        total = (own_ref[rows, :].astype(F32) + term.astype(F32)) * scale
        if half == 0:
            for x in range(4):
                over_x_ref[x, pl.ds(pl.multiple_of(step * 96, 96), 96), :] = total[x * 96:(x + 1) * 96]
        else:
            over_y_ref[0, 0:384, :] = total
    over_y_ref[0, 384:392, :] = up
    over_y_ref[0, 392:400, :] = down

    @pl.when(step == 0)
    def _():
        for x in range(4):
            over_x_ref[x, 384:392, :] = up
            over_x_ref[x, 392:400, :] = down


def pair_sums(mine, theirs, acts, own):
    cols = pl.BlockSpec((784, TOK), lambda i: (0, 0))
    return pl.pallas_call(
        pair_kernel,
        grid=(4,),
        out_shape=[jax.ShapeDtypeStruct((4, 400, 768), F32)] * 2,
        in_specs=[cols, cols, pl.BlockSpec((TOK, 768), lambda i: (0, i)), pl.BlockSpec((768, 768), lambda i: (0, i))],
        out_specs=[pl.BlockSpec((4, 400, 768), lambda i: (0, 0, 0)), pl.BlockSpec((1, 400, 768), lambda i: (i, 0, 0))],
        compiler_params=pltpu.CompilerParams(vmem_limit_bytes=40 << 20),
        cost_estimate=pl.CostEstimate(flops=2 * 768 * TOK * D, bytes_accessed=18 << 20, transcendentals=0),
    )(mine, theirs, acts, own)


def add_parts(parts, rows, top):
    total, up, down = 0.0, None, None
    for part in parts:
        one_up = part[rows:rows + 1].astype(F32)
        one_down = part[rows + 8:rows + 9].astype(F32)
        total = total + part[:rows].astype(F32) * (eighth(one_up) * (1.0 / top))
        up = one_up if up is None else jnp.maximum(up, one_up)
        down = one_down if down is None else jnp.minimum(down, one_down)
    return total, up, down


def code(total, up, down, top):
    value = (total * (eighth(down) * top)).astype(F16).reshape(4, 96, 768)
    up = jnp.broadcast_to(up.astype(F16), (4, 8, 768))
    down = jnp.broadcast_to(down.astype(F16), (4, 8, 768))
    return jnp.concatenate([value, up, down], axis=1)


def local(acts, grads, master, first, second):
    core = lax.axis_index("c")
    x = lax.axis_index("x")
    y = lax.axis_index("y")

    their_acts = swap(acts, "c")
    mine, other = arrange(core, grads, acts)
    their_cols = swap(other, "c")
    own = own_terms(mine, acts)
    over_x, over_y = pair_sums(mine, their_cols, their_acts, own)
    from_x, from_y = [pick(over_x, x)], [pick(over_y, y)]
    for step in (2, 1, 3):
        from_x.append(shift(pick(over_x, (x + step) % 4).astype(F16), "x", step))
        from_y.append(shift(pick(over_y, (y + step) % 4).astype(F16), "y", step))

    send = code(*add_parts(from_x, 384, 2.0 ** 15), 2.0 ** 13)
    part = trade(send, "y")
    low = add_parts([part[i] for i in range(4)], 96, 2.0 ** 13)

    send = code(*add_parts(from_y, 384, 2.0 ** 15), 2.0 ** 13)
    parts = [pick(send, x)]
    for step in (2, 1, 3):
        parts.append(shift(pick(send, (x + step) % 4), "x", step))
    high = add_parts(parts, 96, 2.0 ** 13)

    tile = jnp.concatenate([low[0], high[0]], axis=0)
    up, down = jnp.maximum(low[1], high[1]), jnp.minimum(low[2], high[2])
    send = (tile * (eighth(down) * 2.0 ** 11)).astype(F16)
    send = send.reshape(4, 48, 4, 192).transpose(0, 2, 1, 3).reshape(16, 48, 192)
    up = jnp.broadcast_to(up[:, :64].astype(F16), (16, 48, 64))
    part = trade(jnp.concatenate([send, up], axis=2), ("zh", "zl"))
    up = part[:, :1, 192:193].astype(F32)
    grad = jnp.sum(part[:, :, :192].astype(F32) * (eighth(up) * 2.0 ** -11), axis=0)

    square = jnp.sum(grad * grad)
    square = square + swap(square, "c")
    square = jnp.sum(spread(square, ("x", "y"), 16))
    square = jnp.sum(spread(square, ("zh", "zl"), 16))
    rms = jnp.sqrt(square / (D * FO) + 1e-06)
    clip = jnp.minimum(1.0, 1.0 / rms)
    clipped = clip * grad.T
    new_first = 0.9 * first + 0.1 * clipped
    new_second = 0.95 * second + 0.05 * clipped * clipped
    new_master = master - 0.01 * (new_first / (jnp.sqrt(new_second) + 1e-08) + 0.1 * master)

    params = new_master.astype(BF16).T
    params = trade(jnp.broadcast_to(params, (4, 48, 192)), "zh")
    params = trade(jnp.broadcast_to(params, (4, 4, 48, 192)), "x").reshape(16, 48, 192)
    params = lax.all_gather(params, "c", axis=1, tiled=False)
    return (new_master, new_first, new_second, params.reshape(FO, 192).T)


def solution(mesh):
    fine = Mesh(mesh.devices.reshape(4, 4, 2, 4, 4), ("x", "zh", "c", "y", "zl"))
    dp, seq = ("x", "zh", "c"), ("y", "zl")
    return jax.shard_map(
        local,
        mesh=fine,
        in_specs=(P(dp + seq, None), P(dp + seq, None), P(seq, dp), P(seq, dp), P(seq, dp)),
        out_specs=(P(seq, dp), P(seq, dp), P(seq, dp), P(seq, None)),
        check_vma=False,
    )
```

time: 519 us -> 202 us (0.39)
  blocking collectives: 372 us -> 89.8 us
  waiting for transfers between devices: 117 us -> 13.3 us
  starting transfers between devices: 0.04 us -> 57.9 us
  other arithmetic: 3.49 us -> 18.7 us
  Pallas kernels: 0 us -> 11.7 us
  between operations: 14.7 us -> 3.19 us
  matrix products: 6.6 us -> 0 us
    all_to_all x1 -> x5, blocking collectives: 216 us -> 81.3 us  [trade(): return lax.all_to_all(value, axes, 0, 0, tiled=True)]
    unnamed x2 -> x0, waiting for transfers between devices: 117 us -> none
    psum x1 -> x0, blocking collectives: 102 us -> none  [local(): total_sq = lax.psum(jnp.sum(grad_shard * grad_shard), ('dp', 'seq'))]
    ppermute x0 -> x12, starting transfers between devices: none -> 54.4 us  [the longest x9 32.5 us: shift(): return lax.ppermute(value, axis, [(i, (i + step) % 4) for i in range(4)])]
    all_gather x1, blocking collectives: 54.3 us -> 8.58 us  [local(): params = lax.all_gather(params, 'c', axis=1, tiled=False)]
    pallas_call x0 -> x3, Pallas kernels: none -> 11.7 us  [the longest x1 6.55 us: pair_sums(): pl.pallas_call(pair_kernel, grid=(4,), out_shape=[jax.ShapeDtypeStruct((4...]
    convert_element_type x1 -> x13, other arithmetic: 1.54 us -> 11.7 us  [the longest x1 4.04 us: local(): from_y.append(shift(pick(over_y, (y + step) % 4).astype(F16), 'y', step))]
    all_to_all x0 -> x1, waiting for transfers between devices: none -> 7.66 us  [trade(): return lax.all_to_all(value, axes, 0, 0, tiled=True)]
  transfers between devices with their start and end apart: 1 -> 13, of which waited for: 1 -> 4; matrix products, arithmetic and copies ran while one was open for 0% -> 6% of each run, Pallas kernels for 0% -> 3%
where the time goes in v1:
time: 202 us; the launch traced here: 201 us
  blocking collectives  89.8 us (44%)
  starting transfers between devices  57.9 us (29%)
  other arithmetic  18.7 us (9%)
  waiting for transfers between devices  13.3 us (7%)
  Pallas kernels  11.7 us (6%)
  local copies, waits for them, and re-layouts  5.96 us (3%)
  between operations  3.19 us (2%)
    all_to_all x5, blocking collectives, trade(): return lax.all_to_all(value, axes, 0, 0, tiled=True)  81.3 us
    ppermute x9, starting transfers between devices, shift(): return lax.ppermute(value, axis, [(i, (i + step) % 4) for i in range(4)])  32.5 us
    ppermute x3, starting transfers between devices, swap(): return lax.ppermute(value, axis, [(0, 1), (1, 0)])  21.9 us
    all_gather x1, blocking collectives, local(): params = lax.all_gather(params, 'c', axis=1, tiled=False)  8.58 us
    all_to_all x1, waiting for transfers between devices, trade(): return lax.all_to_all(value, axes, 0, 0, tiled=True)  7.66 us
    pallas_call x1, Pallas kernels, pair_sums(): pl.pallas_call(pair_kernel, grid=(4,), out_shape=[jax.ShapeDtypeStruct((4...  6.55 us
    ppermute x9, waiting for transfers between devices, shift(): return lax.ppermute(value, axis, [(i, (i + step) % 4) for i in range(4)])  4.67 us
    unnamed x16, local copies, waits for them, and re-layouts  4.12 us
  transfers between devices with their start and end apart: 13, of which 4 were waited for; matrix products, arithmetic and copies ran while one was open for 6% of the time, Pallas kernels for 3%

profile of v1, /device:TPU:1, one launch (start us, length us, event | category | flops | bytes accessed | tf_op | source)
XLA Modules:
  0.0 200.6 jit_solution(7615492545557263338)
XLA Ops:
  0.6 8.8 %collective-permute-start.1 = (bf16[384,3072]{1,0:T(8,128)(2,1)}, bf16[384,3072]{1,0:T(8,128)(2,1)}, u32[]{:S(2)}, u32[]{:S(2)}) collective-permute-start(bf16[384,3072]{1,0:T(8,128)(2,1)} %acts_ref.3), channel_id=1, source_target_pairs={{0,16},{16,0},{1,17},{17,1},{2,18},{18,2},{3,19},{19,3},{4,20},{20... | collective-permute-start | bytes 7077896 | tf_op jit(solution)/shard_map/ppermute | solution.py:17
  9.4 1.7 copy-done
  11.1 1.3 copy-done.3
  12.4 1.5 shard_map.84
  13.9 1.9 collective-permute-start
  15.9 3.6 %shard_map.85.own_ref = bf16[768,3072]{1,0:T(8,128)(2,1)S(1)} custom-call(bf16[784,384]{1,0:T(8,128)(2,1)S(1)} %get-tuple-element.8.cols_ref.mine_ref, bf16[384,3072]{1,0:T(8,128)(2,1)S(1)} %copy-done.1), custom_call_target="tpu_custom_call" | custom-call | flops 1811939328 | bytes 8388608 | tf_op jit(solution)/shard_map/pallas_call | solution.py:89
  19.5 0.0 collective-permute-done.their_ref
  19.5 0.0 collective-permute-done.1.acts_ref
  19.5 6.6 %shard_map.86 = (f32[4,400,768]{2,1,0:T(8,128)S(1)}, f32[4,400,768]{2,1,0:T(8,128)}) custom-call(bf16[784,384]{1,0:T(8,128)(2,1)S(1)} %get-tuple-element.8.cols_ref.mine_ref, bf16[784,384]{1,0:T(8,128)(2,1)} %collective-permute-done.their_ref, bf16[384,3072]{1,0:T(8,128)(2,1)} %collective-permute-done.1.acts_ref, bf16[768,3072]{1,0:T(8,128)(2,1)S(1)} %shard_map.85.own_ref), custom_call_target="tpu_custom_call" | custom-call | flops 1811939328 | bytes 18874368 | tf_op jit(solution)/shard_map/pallas_call | solution.py:136
  26.1 4.0 %fusion.15 = (f16[400,768]{1,0:T(8,128)(2,1)S(1)}, f16[400,768]{1,0:T(8,128)(2,1)S(1)}, f16[400,768]{1,0:T(8,128)(2,1)S(1)}) fusion(f32[4,400,768]{2,1,0:T(8,128)} %get-tuple-element.11, s32[]{:T(128)S(6)} %select_n.72, s32[]{:T(128)S(6)} %select_n.76, s32[]{:T(128)S(6)} %select_n.74), kind=kLoop, calls=%fused_computation.27 | loop fusion | flops 921600 | bytes 5529612 | tf_op jit(solution)/shard_map/convert_element_type | solution.py:178
  30.1 1.9 collective-permute-start.7
  32.0 3.4 %collective-permute-start.6 = (f16[400,768]{1,0:T(8,128)(2,1)S(1)}, f16[400,768]{1,0:T(8,128)(2,1)S(1)}, u32[]{:S(2)}, u32[]{:S(2)}) collective-permute-start(f16[400,768]{1,0:T(8,128)(2,1)S(1)} %get-tuple-element.61), channel_id=1, source_target_pairs={{0,4},{4,8},{8,12},{12,0},{1,5},{5,9},{9,13},{13,1},{2,6},{6,10},{... | collective-permute-start | bytes 1843208 | tf_op jit(solution)/shard_map/ppermute | solution.py:21
  35.4 1.9 collective-permute-start.5
  37.4 2.3 %fusion.12 = (f16[400,768]{1,0:T(8,128)(2,1)S(1)}, f16[400,768]{1,0:T(8,128)(2,1)S(1)}, f16[400,768]{1,0:T(8,128)(2,1)S(1)}) fusion(f32[4,400,768]{2,1,0:T(8,128)} %copy-done.2, s32[]{:T(128)S(6)} %select_n.65, s32[]{:T(128)S(6)} %select_n.69, s32[]{:T(128)S(6)} %select_n.67), kind=kLoop, calls=%fused_computation.24 | loop fusion | flops 921600 | bytes 5529612 | tf_op jit(solution)/shard_map/convert_element_type | solution.py:177
  39.7 1.9 collective-permute-start.4
  41.6 3.4 %collective-permute-start.3 = (f16[400,768]{1,0:T(8,128)(2,1)S(1)}, f16[400,768]{1,0:T(8,128)(2,1)S(1)}, u32[]{:S(2)}, u32[]{:S(2)}) collective-permute-start(f16[400,768]{1,0:T(8,128)(2,1)S(1)} %get-tuple-element.58), channel_id=1, source_target_pairs={{0,128},{128,256},{256,384},{384,0},{1,129},{129,257},{257,385},{3... | collective-permute-start | bytes 1843208 | tf_op jit(solution)/shard_map/ppermute | solution.py:21
  45.0 0.8 multiply_reduce_fusion.15
  45.7 1.2 collective-permute-done.7
  46.9 12.8 %collective-permute-start.2 = (f16[400,768]{1,0:T(8,128)(2,1)S(1)}, f16[400,768]{1,0:T(8,128)(2,1)S(1)}, u32[]{:S(2)}, u32[]{:S(2)}) collective-permute-start(f16[400,768]{1,0:T(8,128)(2,1)S(1)} %get-tuple-element.56), channel_id=1, source_target_pairs={{0,256},{128,384},{256,0},{384,128},{1,257},{129,385},{257,1},{385... | collective-permute-start | bytes 1843208 | tf_op jit(solution)/shard_map/ppermute | solution.py:21
  59.8 3.5 %collective-permute-done.6 = f16[400,768]{1,0:T(8,128)(2,1)S(1)} collective-permute-done((f16[400,768]{1,0:T(8,128)(2,1)S(1)}, f16[400,768]{1,0:T(8,128)(2,1)S(1)}, u32[]{:S(2)}, u32[]{:S(2)}) %collective-permute-start.6) | collective-permute-done | bytes 614432 | tf_op jit(solution)/shard_map/ppermute | solution.py:21
  63.2 0.8 convert_reduce_fusion.1
  64.0 0.8 multiply_reduce_fusion.11
  64.9 1.9 fusion.5
  66.8 0.2 pad_maximum_fusion.1
  67.0 0.1 dynamic-slice_bitcast_fusion.4
  67.2 1.9 collective-permute-start.10
  69.1 3.4 %collective-permute-start.9 = (f16[112,768]{1,0:T(8,128)(2,1)S(1)}, f16[112,768]{1,0:T(8,128)(2,1)S(1)}, u32[]{:S(2)}, u32[]{:S(2)}) collective-permute-start(f16[112,768]{1,0:T(8,128)(2,1)S(1)} %get-tuple-element.65), channel_id=1, source_target_pairs={{0,128},{128,256},{256,384},{384,0},{1,129},{129,257},{257,385},{3... | collective-permute-start | bytes 516104 | tf_op jit(solution)/shard_map/ppermute | solution.py:21
  72.5 1.9 collective-permute-start.8
  74.4 0.0 collective-permute-done.3
  74.4 0.8 multiply_reduce_fusion.16
  75.2 0.8 convert_reduce_fusion.3
  76.0 1.8 fusion.11
  77.9 1.1 pad_maximum_fusion
  78.9 3.5 %all-to-all-start = ((f16[4,112,768]{2,1,0:T(8,128)(2,1)}), f16[4,112,768]{2,1,0:T(8,128)(2,1)S(1)}, u32[]{:S(2)}, u32[]{:S(2)}) async-start(f16[4,112,768]{2,1,0:T(8,128)(2,1)} %pad_maximum_fusion), calls=%async_computation | async-start | bytes 1376256 | tf_op jit(solution)/shard_map/all_to_all | solution.py:25
  82.5 0.0 collective-permute-done.10
  82.5 0.0 collective-permute-done.9
  82.6 7.7 %all-to-all-done = f16[4,112,768]{2,1,0:T(8,128)(2,1)S(1)} async-done(((f16[4,112,768]{2,1,0:T(8,128)(2,1)}), f16[4,112,768]{2,1,0:T(8,128)(2,1)S(1)}, u32[]{:S(2)}, u32[]{:S(2)}) %all-to-all-start) | async-done | bytes 688160 | tf_op jit(solution)/shard_map/all_to_all | solution.py:25
  90.3 0.1 multiply_reduce_fusion.7
  90.3 0.1 fusion.21
  90.5 0.1 fusion.22
  90.6 0.6 concatenate.17
  91.2 0.1 mul.785
  91.3 0.2 fusion.18
  91.5 0.1 copy.34
  91.6 0.1 pad.1.clone
  91.7 0.1 pad_maximum_fusion.3
  91.8 28.7 %all_to_all.30 = f16[16,48,256]{2,1,0:T(8,128)(2,1)S(1)} all-to-all(f16[16,48,256]{2,1,0:T(8,128)(2,1)S(1)} %pad_maximum_fusion.3), channel_id=1, replica_groups=mesh['x'=4,'zh'=4,'c'=2,'y'=4,'zl'=4] {'zh','zl'}, dimensions={0} | all-to-all | bytes 786432 | tf_op jit(solution)/shard_map/all_to_all | solution.py:25
  120.5 0.1 slice.313
  120.6 0.1 copy.42
  120.7 0.2 multiply_reduce_fusion
  120.9 0.6 multiply_reduce_fusion.1
  121.5 11.2 %collective-permute-start.11 = (f32[]{:T(128)}, f32[]{:T(128)}, u32[]{:S(2)}, u32[]{:S(2)}) collective-permute-start(f32[]{:T(128)} %multiply_reduce_fusion.1), channel_id=1, source_target_pairs={{0,16},{16,0},{1,17},{17,1},{2,18},{18,2},{3,19},{19,3},{4,20},{20... | collective-permute-start | bytes 20 | tf_op jit(solution)/shard_map/ppermute | solution.py:17
  132.7 0.9 collective-permute-done.11
  135.0 11.1 %all_to_all.31 = f32[16,8,128]{2,1,0:T(8,128)S(1)} all-to-all(f32[16,8,128]{2,1,0:T(8,128)S(1)} %broadcast_in_dim.42), channel_id=1, replica_groups=mesh['x'=4,'zh'=4,'c'=2,'y'=4,'zl'=4] {'x','y'}, dimensions={0} | all-to-all | bytes 131072 | tf_op jit(solution)/shard_map/all_to_all | solution.py:25
  146.1 0.6 slice_reduce_fusion.1
  146.7 0.6 broadcast_in_dim.43
  147.4 17.9 %all_to_all.32 = f32[16,8,128]{2,1,0:T(8,128)S(1)} all-to-all(f32[16,8,128]{2,1,0:T(8,128)S(1)} %broadcast_in_dim.43), channel_id=1, replica_groups=mesh['x'=4,'zh'=4,'c'=2,'y'=4,'zl'=4] {'zh','zl'}, dimensions={0} | all-to-all | bytes 131072 | tf_op jit(solution)/shard_map/all_to_all | solution.py:25
  165.3 0.6 slice_reduce_fusion
  166.6 0.7 convert_bitcast_fusion
  167.3 14.9 %all_to_all.33 = bf16[4,48,192]{2,1,0:T(8,128)(2,1)S(1)} all-to-all(bf16[4,48,192]{2,1,0:T(8,128)(2,1)S(1)} %broadcast_in_dim.44), channel_id=1, replica_groups=mesh['x'=4,'zh'=4,'c'=2,'y'=4,'zl'=4] {'zh'}, dimensions={0} | all-to-all | bytes 147456 | tf_op jit(solution)/shard_map/all_to_all | solution.py:25
  182.2 8.6 %all_to_all.34 = bf16[4,4,48,192]{3,2,1,0:T(8,128)(2,1)S(1)} all-to-all(bf16[4,4,48,192]{3,2,1,0:T(8,128)(2,1)S(1)} %broadcast_in_dim.45), channel_id=1, replica_groups=mesh['x'=4,'zh'=4,'c'=2,'y'=4,'zl'=4] {'x'}, dimensions={0} | all-to-all | bytes 589824 | tf_op jit(solution)/shard_map/all_to_all | solution.py:25
  190.9 8.6 %all_gather.3 = bf16[16,2,48,192]{3,2,0,1:T(8,128)(2,1)S(1)} all-gather(bf16[16,1,48,192]{3,2,0,1:T(8,128)(2,1)S(1)} %bitcast.159), channel_id=1, replica_groups=mesh['x'=4,'zh'=4,'c'=2,'y'=4,'zl'=4] {'c'}, dimensions={1}, use_global_device_ids=true | all-gather | bytes 884736 | tf_op jit(solution)/shard_map/all_gather | solution.py:213
  199.4 0.1 copy.38
  199.5 1.1 copy.39
  (34 shorter events, 0.3 us)
Async XLA Ops:
  0.6 18.9 %collective-permute-start.1 = (bf16[384,3072]{1,0:T(8,128)(2,1)}, bf16[384,3072]{1,0:T(8,128)(2,1)}, u32[]{:S(2)}, u32[]{:S(2)}) collective-permute-start(bf16[384,3072]{1,0:T(8,128)(2,1)} %acts_ref.3), channel_id=1, source_target_pairs={{0,16},{16,0},{1,17},{17,1},{2,18},{18,2},{3,19},{19,3},{4,20},{20... | collective-permute-start | bytes 7077896 | tf_op jit(solution)/shard_map/ppermute | solution.py:17
  9.4 1.7 copy-start
  11.1 1.3 copy-start.3
  12.4 3.5 %copy-start.1 = (bf16[384,3072]{1,0:T(8,128)(2,1)S(1)}, bf16[384,3072]{1,0:T(8,128)(2,1)}, u32[]{:S(2)}) copy-start(bf16[384,3072]{1,0:T(8,128)(2,1)} %acts_ref.3) | copy-start | bytes 7077892
  13.9 5.6 %collective-permute-start = (bf16[784,384]{1,0:T(8,128)(2,1)}, bf16[784,384]{1,0:T(8,128)(2,1)}, u32[]{:S(2)}, u32[]{:S(2)}) collective-permute-start(bf16[784,384]{1,0:T(8,128)(2,1)} %get-tuple-element.9), channel_id=1, source_target_pairs={{0,16},{16,0},{1,17},{17,1},{2,18},{18,2},{3,19},{19,3},{4,20},{20... | collective-permute-start | bytes 1806344 | tf_op jit(solution)/shard_map/ppermute | solution.py:17
  26.1 4.0 %copy-start.2 = (f32[4,400,768]{2,1,0:T(8,128)}, f32[4,400,768]{2,1,0:T(8,128)S(1)}, u32[]{:S(2)}) copy-start(f32[4,400,768]{2,1,0:T(8,128)S(1)} %get-tuple-element.10) | copy-start | bytes 14745604
  30.1 16.8 %collective-permute-start.7 = (f16[400,768]{1,0:T(8,128)(2,1)S(1)}, f16[400,768]{1,0:T(8,128)(2,1)S(1)}, u32[]{:S(2)}, u32[]{:S(2)}) collective-permute-start(f16[400,768]{1,0:T(8,128)(2,1)S(1)} %get-tuple-element.60), channel_id=1, source_target_pairs={{0,12},{4,0},{8,4},{12,8},{1,13},{5,1},{9,5},{13,9},{2,14},{6,2},{... | collective-permute-start | bytes 1843208 | tf_op jit(solution)/shard_map/ppermute | solution.py:21
  32.0 31.2 %collective-permute-start.6 = (f16[400,768]{1,0:T(8,128)(2,1)S(1)}, f16[400,768]{1,0:T(8,128)(2,1)S(1)}, u32[]{:S(2)}, u32[]{:S(2)}) collective-permute-start(f16[400,768]{1,0:T(8,128)(2,1)S(1)} %get-tuple-element.61), channel_id=1, source_target_pairs={{0,4},{4,8},{8,12},{12,0},{1,5},{5,9},{9,13},{13,1},{2,6},{6,10},{... | collective-permute-start | bytes 1843208 | tf_op jit(solution)/shard_map/ppermute | solution.py:21
  35.4 27.8 %collective-permute-start.5 = (f16[400,768]{1,0:T(8,128)(2,1)S(1)}, f16[400,768]{1,0:T(8,128)(2,1)}, u32[]{:S(2)}, u32[]{:S(2)}) collective-permute-start(f16[400,768]{1,0:T(8,128)(2,1)S(1)} %get-tuple-element.59), channel_id=1, source_target_pairs={{0,8},{4,12},{8,0},{12,4},{1,9},{5,13},{9,1},{13,5},{2,10},{6,14},... | collective-permute-start | bytes 1843208 | tf_op jit(solution)/shard_map/ppermute | solution.py:21
  39.7 32.8 %collective-permute-start.4 = (f16[400,768]{1,0:T(8,128)(2,1)S(1)}, f16[400,768]{1,0:T(8,128)(2,1)S(1)}, u32[]{:S(2)}, u32[]{:S(2)}) collective-permute-start(f16[400,768]{1,0:T(8,128)(2,1)S(1)} %get-tuple-element.57), channel_id=1, source_target_pairs={{0,384},{128,0},{256,128},{384,256},{1,385},{129,1},{257,129},{385... | collective-permute-start | bytes 1843208 | tf_op jit(solution)/shard_map/ppermute | solution.py:21
  41.6 32.8 %collective-permute-start.3 = (f16[400,768]{1,0:T(8,128)(2,1)S(1)}, f16[400,768]{1,0:T(8,128)(2,1)S(1)}, u32[]{:S(2)}, u32[]{:S(2)}) collective-permute-start(f16[400,768]{1,0:T(8,128)(2,1)S(1)} %get-tuple-element.58), channel_id=1, source_target_pairs={{0,128},{128,256},{256,384},{384,0},{1,129},{129,257},{257,385},{3... | collective-permute-start | bytes 1843208 | tf_op jit(solution)/shard_map/ppermute | solution.py:21
  46.9 27.5 %collective-permute-start.2 = (f16[400,768]{1,0:T(8,128)(2,1)S(1)}, f16[400,768]{1,0:T(8,128)(2,1)S(1)}, u32[]{:S(2)}, u32[]{:S(2)}) collective-permute-start(f16[400,768]{1,0:T(8,128)(2,1)S(1)} %get-tuple-element.56), channel_id=1, source_target_pairs={{0,256},{128,384},{256,0},{384,128},{1,257},{129,385},{257,1},{385... | collective-permute-start | bytes 1843208 | tf_op jit(solution)/shard_map/ppermute | solution.py:21
  67.2 15.3 %collective-permute-start.10 = (f16[112,768]{1,0:T(8,128)(2,1)S(1)}, f16[112,768]{1,0:T(8,128)(2,1)S(1)}, u32[]{:S(2)}, u32[]{:S(2)}) collective-permute-start(f16[112,768]{1,0:T(8,128)(2,1)S(1)} %get-tuple-element.64), channel_id=1, source_target_pairs={{0,384},{128,0},{256,128},{384,256},{1,385},{129,1},{257,129},{385... | collective-permute-start | bytes 516104 | tf_op jit(solution)/shard_map/ppermute | solution.py:21
  69.1 13.4 %collective-permute-start.9 = (f16[112,768]{1,0:T(8,128)(2,1)S(1)}, f16[112,768]{1,0:T(8,128)(2,1)S(1)}, u32[]{:S(2)}, u32[]{:S(2)}) collective-permute-start(f16[112,768]{1,0:T(8,128)(2,1)S(1)} %get-tuple-element.65), channel_id=1, source_target_pairs={{0,128},{128,256},{256,384},{384,0},{1,129},{129,257},{257,385},{3... | collective-permute-start | bytes 516104 | tf_op jit(solution)/shard_map/ppermute | solution.py:21
  72.5 10.1 %collective-permute-start.8 = (f16[112,768]{1,0:T(8,128)(2,1)S(1)}, f16[112,768]{1,0:T(8,128)(2,1)S(1)}, u32[]{:S(2)}, u32[]{:S(2)}) collective-permute-start(f16[112,768]{1,0:T(8,128)(2,1)S(1)} %get-tuple-element.63), channel_id=1, source_target_pairs={{0,256},{128,384},{256,0},{384,128},{1,257},{129,385},{257,1},{385... | collective-permute-start | bytes 516104 | tf_op jit(solution)/shard_map/ppermute | solution.py:21
  78.9 11.3 %all-to-all-start = ((f16[4,112,768]{2,1,0:T(8,128)(2,1)}), f16[4,112,768]{2,1,0:T(8,128)(2,1)S(1)}, u32[]{:S(2)}, u32[]{:S(2)}) async-start(f16[4,112,768]{2,1,0:T(8,128)(2,1)} %pad_maximum_fusion), calls=%async_computation | async-start | bytes 1376256 | tf_op jit(solution)/shard_map/all_to_all | solution.py:25
  91.7 74.9 %copy-start.4 = (f32[192,48]{0,1:T(8,128)S(1)}, f32[192,48]{0,1:T(8,128)}, u32[]{:S(2)}) copy-start(f32[192,48]{0,1:T(8,128)} %param.7) | copy-start | bytes 110596
  91.7 74.9 %copy-start.5 = (f32[192,48]{0,1:T(8,128)S(1)}, f32[192,48]{0,1:T(8,128)}, u32[]{:S(2)}) copy-start(f32[192,48]{0,1:T(8,128)} %param.9) | copy-start | bytes 110596
  91.7 74.9 %copy-start.6 = (f32[192,48]{0,1:T(8,128)S(1)}, f32[192,48]{0,1:T(8,128)}, u32[]{:S(2)}) copy-start(f32[192,48]{0,1:T(8,128)} %param.8) | copy-start | bytes 110596
  121.5 12.1 %collective-permute-start.11 = (f32[]{:T(128)}, f32[]{:T(128)}, u32[]{:S(2)}, u32[]{:S(2)}) collective-permute-start(f32[]{:T(128)} %multiply_reduce_fusion.1), channel_id=1, source_target_pairs={{0,16},{16,0},{1,17},{17,1},{2,18},{18,2},{3,19},{19,3},{4,20},{20... | collective-permute-start | bytes 20 | tf_op jit(solution)/shard_map/ppermute | solution.py:17

commit v2 on v1

--- a/solution.py
+++ b/solution.py
@@ -44,7 +44,7 @@
         for x in range(4):
             block = grads_ref[:, x * 384:(x + 1) * 384].T
             for zh in range(4):
-                to = (zh // 2) * 384 + x * 96 + (zh % 2) * 48
+                to = x * 192 + zh * 48
                 even_ref[to:to + 48, :] = block[zh * 96:zh * 96 + 48]
                 odd_ref[to:to + 48, :] = block[zh * 96 + 48:zh * 96 + 96]
 
@@ -97,8 +97,9 @@
     )(cols, acts)
 
 
-def pair_kernel(mine_ref, their_ref, acts_ref, own_ref, over_x_ref, over_y_ref):
+def pair_kernel(core_ref, mine_ref, their_ref, acts_ref, own_ref, out_ref):
     step = pl.program_id(0)
+    core = core_ref[0]
     bound = jnp.zeros((16, 128), F32)
     for ref in (mine_ref, their_ref):
         bound = bound + TOK * ref[768:784, 0:128].astype(F32) * ref[768:784, 128:256].astype(F32)
@@ -109,39 +110,41 @@
         up = jnp.where(over, up * 2.0, up)
         down = jnp.where(over, down * 0.5, down)
     scale = eighth(down[0:1, 0:1]) * 2.0 ** 15
-    up = jnp.broadcast_to(up[0:1, 0:1], (8, 768))
-    down = jnp.broadcast_to(down[0:1, 0:1], (8, 768))
 
     for half in range(2):
         rows = slice(384 * half, 384 * (half + 1))
         term = jnp.dot(their_ref[rows, :], acts_ref[...], preferred_element_type=F32).astype(BF16)
         total = (own_ref[rows, :].astype(F32) + term.astype(F32)) * scale
-        if half == 0:
-            for x in range(4):
-                over_x_ref[x, pl.ds(pl.multiple_of(step * 96, 96), 96), :] = total[x * 96:(x + 1) * 96]
-        else:
-            over_y_ref[0, 0:384, :] = total
-    over_y_ref[0, 384:392, :] = up
-    over_y_ref[0, 392:400, :] = down
+        for part in range(2):
+            x = 2 * half + part
+            u = jnp.where(core == 0, x, step)
+            v = jnp.where(core == 0, step, x)
+            out_ref[u, pl.ds(pl.multiple_of(v * 192, 192), 192), :] = total[part * 192:(part + 1) * 192]
 
     @pl.when(step == 0)
     def _():
-        for x in range(4):
-            over_x_ref[x, 384:392, :] = up
-            over_x_ref[x, 392:400, :] = down
-
-
-def pair_sums(mine, theirs, acts, own):
+        for u in range(4):
+            out_ref[u, 768:776, :] = jnp.broadcast_to(up[0:1, 0:1], (8, 768))
+            out_ref[u, 776:784, :] = jnp.broadcast_to(down[0:1, 0:1], (8, 768))
+
+
+def pair_sums(core, mine, theirs, acts, own):
     cols = pl.BlockSpec((784, TOK), lambda i: (0, 0))
     return pl.pallas_call(
         pair_kernel,
         grid=(4,),
-        out_shape=[jax.ShapeDtypeStruct((4, 400, 768), F32)] * 2,
-        in_specs=[cols, cols, pl.BlockSpec((TOK, 768), lambda i: (0, i)), pl.BlockSpec((768, 768), lambda i: (0, i))],
-        out_specs=[pl.BlockSpec((4, 400, 768), lambda i: (0, 0, 0)), pl.BlockSpec((1, 400, 768), lambda i: (i, 0, 0))],
+        out_shape=jax.ShapeDtypeStruct((4, 784, 768), F32),
+        in_specs=[
+            pl.BlockSpec(memory_space=pltpu.SMEM),
+            cols,
+            cols,
+            pl.BlockSpec((TOK, 768), lambda i: (0, i)),
+            pl.BlockSpec((768, 768), lambda i: (0, i)),
+        ],
+        out_specs=pl.BlockSpec((4, 784, 768), lambda i: (0, 0, 0)),
         compiler_params=pltpu.CompilerParams(vmem_limit_bytes=40 << 20),
         cost_estimate=pl.CostEstimate(flops=2 * 768 * TOK * D, bytes_accessed=18 << 20, transcendentals=0),
-    )(mine, theirs, acts, own)
+    )(core.reshape(1), mine, theirs, acts, own)
 
 
 def add_parts(parts, rows, top):
@@ -156,10 +159,39 @@
 
 
 def code(total, up, down, top):
-    value = (total * (eighth(down) * top)).astype(F16).reshape(4, 96, 768)
+    value = (total * (eighth(down) * top)).astype(F16).reshape(4, 192, 768)
     up = jnp.broadcast_to(up.astype(F16), (4, 8, 768))
     down = jnp.broadcast_to(down.astype(F16), (4, 8, 768))
     return jnp.concatenate([value, up, down], axis=1)
+
+
+def z_kernel(tile_ref, up_ref, down_ref, out_ref):
+    scale = eighth(down_ref[0:1, 0:1]) * 2.0 ** 11
+    for zh in range(4):
+        for zl in range(4):
+            piece = tile_ref[zh * 48:(zh + 1) * 48, zl * 192:(zl + 1) * 192]
+            out_ref[zh * 4 + zl, :, 0:192] = piece * scale
+            out_ref[zh * 4 + zl, :, 192:256] = jnp.broadcast_to(up_ref[0:1, 0:1], (48, 64))
+
+
+def z_pieces(tile, up, down):
+    vmem = pl.BlockSpec(memory_space=pltpu.VMEM)
+    return pl.pallas_call(
+        z_kernel,
+        out_shape=jax.ShapeDtypeStruct((16, 48, 256), F32),
+        in_specs=[vmem, vmem, vmem],
+        out_specs=vmem,
+        compiler_params=pltpu.CompilerParams(vmem_limit_bytes=24 << 20),
+    )(tile, up, down)
+
+
+def cross_trade(value, first):
+    groups = []
+    for core in range(2):
+        for a in range(4):
+            fours = [(b, core, a) if core == first else (a, core, b) for b in range(4)]
+            groups.append([(x * 2 + c) * 4 + y for x, c, y in fours])
+    return lax.all_to_all(value, ("x", "c", "y"), 0, 0, axis_index_groups=groups, tiled=True)
 
 
 def local(acts, grads, master, first, second):
@@ -171,34 +203,17 @@
     mine, other = arrange(core, grads, acts)
     their_cols = swap(other, "c")
     own = own_terms(mine, acts)
-    over_x, over_y = pair_sums(mine, their_cols, their_acts, own)
-    from_x, from_y = [pick(over_x, x)], [pick(over_y, y)]
-    for step in (2, 1, 3):
-        from_x.append(shift(pick(over_x, (x + step) % 4).astype(F16), "x", step))
-        from_y.append(shift(pick(over_y, (y + step) % 4).astype(F16), "y", step))
-
-    send = code(*add_parts(from_x, 384, 2.0 ** 15), 2.0 ** 13)
-    part = trade(send, "y")
-    low = add_parts([part[i] for i in range(4)], 96, 2.0 ** 13)
-
-    send = code(*add_parts(from_y, 384, 2.0 ** 15), 2.0 ** 13)
-    parts = [pick(send, x)]
-    for step in (2, 1, 3):
-        parts.append(shift(pick(send, (x + step) % 4), "x", step))
-    high = add_parts(parts, 96, 2.0 ** 13)
-
-    tile = jnp.concatenate([low[0], high[0]], axis=0)
-    up, down = jnp.maximum(low[1], high[1]), jnp.minimum(low[2], high[2])
-    send = (tile * (eighth(down) * 2.0 ** 11)).astype(F16)
-    send = send.reshape(4, 48, 4, 192).transpose(0, 2, 1, 3).reshape(16, 48, 192)
-    up = jnp.broadcast_to(up[:, :64].astype(F16), (16, 48, 64))
-    part = trade(jnp.concatenate([send, up], axis=2), ("zh", "zl"))
+    part = cross_trade(pair_sums(core, mine, their_cols, their_acts, own).astype(F16), 0)
+    send = code(*add_parts([part[i] for i in range(4)], 768, 2.0 ** 15), 2.0 ** 13)
+    part = cross_trade(send, 1)
+    tile, up, down = add_parts([part[i] for i in range(4)], 192, 2.0 ** 13)
+
+    part = trade(z_pieces(tile, up, down).astype(F16), ("zh", "zl"))
     up = part[:, :1, 192:193].astype(F32)
     grad = jnp.sum(part[:, :, :192].astype(F32) * (eighth(up) * 2.0 ** -11), axis=0)
 
     square = jnp.sum(grad * grad)
-    square = square + swap(square, "c")
-    square = jnp.sum(spread(square, ("x", "y"), 16))
+    square = jnp.sum(spread(square, ("x", "y", "c"), 32))
     square = jnp.sum(spread(square, ("zh", "zl"), 16))
     rms = jnp.sqrt(square / (D * FO) + 1e-06)
     clip = jnp.minimum(1.0, 1.0 / rms)
@@ -210,7 +225,8 @@
     params = new_master.astype(BF16).T
     params = trade(jnp.broadcast_to(params, (4, 48, 192)), "zh")
     params = trade(jnp.broadcast_to(params, (4, 4, 48, 192)), "x").reshape(16, 48, 192)
-    params = lax.all_gather(params, "c", axis=1, tiled=False)
+    theirs = swap(params, "c")
+    params = jnp.where(core == 0, jnp.stack([params, theirs], 1), jnp.stack([theirs, params], 1))
     return (new_master, new_first, new_second, params.reshape(FO, 192).T)
 
 

time: 202 us -> 185 us (0.916)
  blocking collectives: 89.8 us -> 135 us
  starting transfers between devices: 57.9 us -> 17.5 us
  waiting for transfers between devices: 13.3 us -> 1.33 us
  other arithmetic: 18.7 us -> 9.43 us
    all_to_all x0 -> x2, blocking collectives: none -> 46.2 us  [cross_trade(): lax.all_to_all(value, ('x', 'c', 'y'), 0, 0, axis_index_groups=groups, ti...]
    ppermute x9 -> x0, starting transfers between devices: 32.5 us -> none  [shift(): return lax.ppermute(value, axis, [(i, (i + step) % 4) for i in range(4)])]
    all_gather x1 -> x0, blocking collectives: 8.58 us -> none  [local(): params = lax.all_gather(params, 'c', axis=1, tiled=False)]
    all_to_all x5, blocking collectives: 81.3 us -> 89 us  [trade(): return lax.all_to_all(value, axes, 0, 0, tiled=True)]
    all_to_all x1 -> x0, waiting for transfers between devices: 7.66 us -> none  [trade(): return lax.all_to_all(value, axes, 0, 0, tiled=True)]
    convert_element_type x11 -> x3, other arithmetic: 11.7 us -> 5.43 us  [the longest x1 4.29 us: local(): pair_sums(core, mine, their_cols, their_acts, own).astype(F16)]
    ppermute x9 -> x0, waiting for transfers between devices: 4.67 us -> none  [shift(): return lax.ppermute(value, axis, [(i, (i + step) % 4) for i in range(4)])]
    ppermute x3, starting transfers between devices: 21.9 us -> 17.5 us  [swap(): return lax.ppermute(value, axis, [(0, 1), (1, 0)])]
  transfers between devices with their start and end apart: 13 -> 3, of which waited for: 4 -> 1; matrix products, arithmetic and copies ran while one was open for 6% -> 0% of each run, Pallas kernels for 3% -> 2%
where the time goes in v2:
time: 185 us; the launch traced here: 184 us
  blocking collectives  135 us (73%)
  starting transfers between devices  17.5 us (9%)
  Pallas kernels  12.4 us (7%)
  other arithmetic  9.43 us (5%)
  local copies, waits for them, and re-layouts  6.59 us (4%)
    all_to_all x5, blocking collectives, trade(): return lax.all_to_all(value, axes, 0, 0, tiled=True)  89 us
    all_to_all x2, blocking collectives, cross_trade(): lax.all_to_all(value, ('x', 'c', 'y'), 0, 0, axis_index_groups=groups, ti...  46.2 us
    ppermute x3, starting transfers between devices, swap(): return lax.ppermute(value, axis, [(0, 1), (1, 0)])  17.5 us
    pallas_call x1, Pallas kernels, pair_sums(): pl.pallas_call(pair_kernel, grid=(4,), out_shape=jax.ShapeDtypeStruct((4,...  7.8 us
    convert_element_type x1, other arithmetic, local(): pair_sums(core, mine, their_cols, their_acts, own).astype(F16)  4.29 us
    unnamed x13, local copies, waits for them, and re-layouts  4.03 us
  transfers between devices with their start and end apart: 3, of which 1 were waited for; matrix products, arithmetic and copies ran while one was open for 0% of the time, Pallas kernels for 2%

profile of v2, /device:TPU:1, one launch (start us, length us, event | category | flops | bytes accessed | tf_op | source)
XLA Modules:
  0.0 183.9 jit_solution(9252430314956320013)
XLA Ops:
  0.6 8.8 %collective-permute-start.1 = (bf16[384,3072]{1,0:T(8,128)(2,1)}, bf16[384,3072]{1,0:T(8,128)(2,1)S(1)}, u32[]{:S(2)}, u32[]{:S(2)}) collective-permute-start(bf16[384,3072]{1,0:T(8,128)(2,1)} %acts_ref.3), channel_id=1, source_target_pairs={{0,16},{16,0},{1,17},{17,1},{2,18},{18,2},{3,19},{19,3},{4,20},{20... | collective-permute-start | bytes 7077896 | tf_op jit(solution)/shard_map/ppermute | solution.py:17
  9.4 0.0 copy-start
  9.4 1.7 copy-done
  11.1 0.0 copy-start.2
  11.1 1.3 copy-done.2
  12.4 0.0 copy-start.1
  12.4 0.7 shard_map.84
  13.1 1.9 %collective-permute-start = (bf16[784,384]{1,0:T(8,128)(2,1)S(1)}, bf16[784,384]{1,0:T(8,128)(2,1)S(1)}, u32[]{:S(2)}, u32[]{:S(2)}) collective-permute-start(bf16[784,384]{1,0:T(8,128)(2,1)S(1)} %get-tuple-element.7), channel_id=1, source_target_pairs={{0,16},{16,0},{1,17},{17,1},{2,18},{18,2},{3,19},{19,3},{4,20},{20... | collective-permute-start | bytes 1806344 | tf_op jit(solution)/shard_map/ppermute | solution.py:17
  15.0 0.0 copy-done.1
  15.0 3.6 %shard_map.85.own_ref = bf16[768,3072]{1,0:T(8,128)(2,1)S(1)} custom-call(bf16[784,384]{1,0:T(8,128)(2,1)S(1)} %get-tuple-element.6.cols_ref.mine_ref, bf16[384,3072]{1,0:T(8,128)(2,1)S(1)} %copy-done.1), custom_call_target="tpu_custom_call" | custom-call | flops 1811939328 | bytes 8388608 | tf_op jit(solution)/shard_map/pallas_call | solution.py:89
  18.6 0.0 collective-permute-done.their_ref
  18.7 0.0 collective-permute-done.1.acts_ref
  18.7 7.8 %shard_map.86 = f32[4,784,768]{2,1,0:T(8,128)} custom-call(s32[1]{0:T(128)} %bitcast.core_ref, bf16[784,384]{1,0:T(8,128)(2,1)S(1)} %get-tuple-element.6.cols_ref.mine_ref, bf16[784,384]{1,0:T(8,128)(2,1)S(1)} %collective-permute-done.their_ref, bf16[384,3072]{1,0:T(8,128)(2,1)S(1)} %collective-permute-done.1.acts_ref, bf16[768,3072]{1,0:T(8,128)(2,1)S(1)} %shard_map.85.own_ref), custom_call_target="tpu_custom_call" | custom-call | flops 1811939328 | bytes 18874368 | tf_op jit(solution)/shard_map/pallas_call | solution.py:133
  26.5 4.3 %convert_element_type.281 = f16[4,784,768]{2,1,0:T(8,128)(2,1)S(1)} convert(f32[4,784,768]{2,1,0:T(8,128)} %shard_map.86) | non-fusion elementwise | flops 2408448 | bytes 14450688 | tf_op jit(solution)/shard_map/convert_element_type | solution.py:206
  30.8 32.5 %all_to_all.35 = f16[4,784,768]{2,1,0:T(8,128)(2,1)S(1)} all-to-all(f16[4,784,768]{2,1,0:T(8,128)(2,1)S(1)} %convert_element_type.281), channel_id=1, replica_groups={{0,128,256,384},{4,132,260,388},{8,136,264,392},{12,140,268,396},{16,20..., dimensions={0} | all-to-all | bytes 9633792 | tf_op jit(solution)/shard_map/all_to_all | solution.py:194
  63.3 0.1 multiply_reduce_fusion.10
  63.4 1.1 fusion.25
  64.5 1.1 fusion.2
  65.7 0.4 pad_maximum_fusion
  66.0 13.7 %all_to_all.36 = f16[4,208,768]{2,1,0:T(8,128)(2,1)S(1)} all-to-all(f16[4,208,768]{2,1,0:T(8,128)(2,1)S(1)} %pad_maximum_fusion), channel_id=1, replica_groups={{0,4,8,12},{128,132,136,140},{256,260,264,268},{384,388,392,396},{16,14..., dimensions={0} | all-to-all | bytes 2555904 | tf_op jit(solution)/shard_map/all_to_all | solution.py:194
  79.7 0.1 fusion.16
  79.8 0.2 fusion.5.tile_ref
  80.0 0.0 copy-start.3
  80.0 0.0 copy-start.4
  80.0 0.0 copy-start.5
  80.1 0.3 shard_map.87
  80.3 0.1 convert_element_type.316
  80.4 27.0 %all_to_all.37 = f16[16,48,256]{2,1,0:T(8,128)(2,1)S(1)} all-to-all(f16[16,48,256]{2,1,0:T(8,128)(2,1)S(1)} %convert_element_type.316), channel_id=1, replica_groups=mesh['x'=4,'zh'=4,'c'=2,'y'=4,'zl'=4] {'zh','zl'}, dimensions={0} | all-to-all | bytes 786432 | tf_op jit(solution)/shard_map/all_to_all | solution.py:25
  107.4 0.3 fusion.14
  107.6 0.2 multiply_reduce_fusion
  107.8 0.6 multiply_reduce_fusion.1
  108.4 0.7 broadcast_in_dim.24
  109.1 20.1 %all_to_all.38 = f32[32,8,128]{2,1,0:T(8,128)S(1)} all-to-all(f32[32,8,128]{2,1,0:T(8,128)S(1)} %broadcast_in_dim.24), channel_id=1, replica_groups=mesh['x'=4,'zh'=4,'c'=2,'y'=4,'zl'=4] {'x','y','c'}, dimensions={0} | all-to-all | bytes 262144 | tf_op jit(solution)/shard_map/all_to_all | solution.py:25
  129.2 0.6 slice_reduce_fusion
  129.8 0.6 broadcast_in_dim.25
  130.5 17.6 %all_to_all.39 = f32[16,8,128]{2,1,0:T(8,128)S(1)} all-to-all(f32[16,8,128]{2,1,0:T(8,128)S(1)} %broadcast_in_dim.25), channel_id=1, replica_groups=mesh['x'=4,'zh'=4,'c'=2,'y'=4,'zl'=4] {'zh','zl'}, dimensions={0} | all-to-all | bytes 131072 | tf_op jit(solution)/shard_map/all_to_all | solution.py:25
  148.1 0.6 slice_reduce_fusion.1
  149.4 0.0 copy-done.3
  149.4 0.0 copy-done.4
  149.4 0.0 copy-done.5
  149.4 0.7 convert_bitcast_fusion
  150.1 15.7 %all_to_all.40 = bf16[4,48,192]{2,1,0:T(8,128)(2,1)S(1)} all-to-all(bf16[4,48,192]{2,1,0:T(8,128)(2,1)S(1)} %broadcast_in_dim.26), channel_id=1, replica_groups=mesh['x'=4,'zh'=4,'c'=2,'y'=4,'zl'=4] {'zh'}, dimensions={0} | all-to-all | bytes 147456 | tf_op jit(solution)/shard_map/all_to_all | solution.py:25
  165.8 8.6 %all_to_all.41 = bf16[4,4,48,192]{3,2,1,0:T(8,128)(2,1)S(1)} all-to-all(bf16[4,4,48,192]{3,2,1,0:T(8,128)(2,1)S(1)} %broadcast_in_dim.27), channel_id=1, replica_groups=mesh['x'=4,'zh'=4,'c'=2,'y'=4,'zl'=4] {'x'}, dimensions={0} | all-to-all | bytes 589824 | tf_op jit(solution)/shard_map/all_to_all | solution.py:25
  174.4 6.7 %collective-permute-start.2 = (bf16[16,48,192]{2,1,0:T(8,128)(2,1)S(1)}, bf16[16,48,192]{2,1,0:T(8,128)(2,1)S(1)}, u32[]{:S(2)}, u32[]{:S(2)}) collective-permute-start(bf16[16,48,192]{2,1,0:T(8,128)(2,1)S(1)} %bitcast.53), channel_id=1, source_target_pairs={{0,16},{16,0},{1,17},{17,1},{2,18},{18,2},{3,19},{19,3},{4,20},{20... | collective-permute-start | bytes 884744 | tf_op jit(solution)/shard_map/ppermute | solution.py:17
  181.2 1.3 collective-permute-done.2
  182.5 0.2 maximum_select_fusion
  182.8 0.1 copy.20
  182.9 1.1 copy.21
  (6 shorter events, 0.1 us)
Async XLA Ops:
  0.6 18.0 %collective-permute-start.1 = (bf16[384,3072]{1,0:T(8,128)(2,1)}, bf16[384,3072]{1,0:T(8,128)(2,1)S(1)}, u32[]{:S(2)}, u32[]{:S(2)}) collective-permute-start(bf16[384,3072]{1,0:T(8,128)(2,1)} %acts_ref.3), channel_id=1, source_target_pairs={{0,16},{16,0},{1,17},{17,1},{2,18},{18,2},{3,19},{19,3},{4,20},{20... | collective-permute-start | bytes 7077896 | tf_op jit(solution)/shard_map/ppermute | solution.py:17
  9.4 1.7 copy-start
  11.1 1.3 copy-start.2
  12.4 2.7 %copy-start.1 = (bf16[384,3072]{1,0:T(8,128)(2,1)S(1)}, bf16[384,3072]{1,0:T(8,128)(2,1)}, u32[]{:S(2)}) copy-start(bf16[384,3072]{1,0:T(8,128)(2,1)} %acts_ref.3) | copy-start | bytes 7077892
  13.1 5.5 %collective-permute-start = (bf16[784,384]{1,0:T(8,128)(2,1)S(1)}, bf16[784,384]{1,0:T(8,128)(2,1)S(1)}, u32[]{:S(2)}, u32[]{:S(2)}) collective-permute-start(bf16[784,384]{1,0:T(8,128)(2,1)S(1)} %get-tuple-element.7), channel_id=1, source_target_pairs={{0,16},{16,0},{1,17},{17,1},{2,18},{18,2},{3,19},{19,3},{4,20},{20... | collective-permute-start | bytes 1806344 | tf_op jit(solution)/shard_map/ppermute | solution.py:17
  80.0 69.4 %copy-start.3 = (f32[192,48]{0,1:T(8,128)S(1)}, f32[192,48]{0,1:T(8,128)}, u32[]{:S(2)}) copy-start(f32[192,48]{0,1:T(8,128)} %param.7) | copy-start | bytes 110596
  80.0 69.4 %copy-start.4 = (f32[192,48]{0,1:T(8,128)S(1)}, f32[192,48]{0,1:T(8,128)}, u32[]{:S(2)}) copy-start(f32[192,48]{0,1:T(8,128)} %param.9) | copy-start | bytes 110596
  80.0 69.4 %copy-start.5 = (f32[192,48]{0,1:T(8,128)S(1)}, f32[192,48]{0,1:T(8,128)}, u32[]{:S(2)}) copy-start(f32[192,48]{0,1:T(8,128)} %param.8) | copy-start | bytes 110596
  174.4 8.1 %collective-permute-start.2 = (bf16[16,48,192]{2,1,0:T(8,128)(2,1)S(1)}, bf16[16,48,192]{2,1,0:T(8,128)(2,1)S(1)}, u32[]{:S(2)}, u32[]{:S(2)}) collective-permute-start(bf16[16,48,192]{2,1,0:T(8,128)(2,1)S(1)} %bitcast.53), channel_id=1, source_target_pairs={{0,16},{16,0},{1,17},{17,1},{2,18},{18,2},{3,19},{19,3},{4,20},{20... | collective-permute-start | bytes 884744 | tf_op jit(solution)/shard_map/ppermute | solution.py:17

commit v3 on v2

v3 whole, which is shorter than its diff:
```python
import functools

import jax
import jax.numpy as jnp
from jax import lax
from jax.experimental import pallas as pl
from jax.experimental.pallas import tpu as pltpu
from jax.sharding import Mesh, PartitionSpec as P

D = 3072
FO = 1536
TOK = 384
F32 = jnp.float32
F16 = jnp.float16
BF16 = jnp.bfloat16


def swap(value, axis):
    return lax.ppermute(value, axis, [(0, 1), (1, 0)])


def trade(value, axes):
    return lax.all_to_all(value, axes, 0, 0, tiled=True)


def eighth(value):
    value = value * value
    value = value * value
    return value * value


def arrange_kernel(core_ref, grads_ref, acts_ref, mine_ref, other_ref):
    def write(even_ref, odd_ref):
        for x in range(4):
            block = grads_ref[:, x * 384:(x + 1) * 384].T
            for zh in range(4):
                to = (zh // 2) * 384 + x * 96 + (zh % 2) * 48
                even_ref[to:to + 48, :] = block[zh * 96:zh * 96 + 48]
                odd_ref[to:to + 48, :] = block[zh * 96 + 48:zh * 96 + 96]

    @pl.when(core_ref[0] == 0)
    def _():
        write(mine_ref, other_ref)

    @pl.when(core_ref[0] != 0)
    def _():
        write(other_ref, mine_ref)

    def peak(ref):
        top = jnp.abs(ref[0:16, :])
        for row in range(16, TOK, 16):
            top = jnp.maximum(top, jnp.abs(ref[row:row + 16, :]))
        return jnp.max(top.astype(F32))

    acts_peak, grads_peak = peak(acts_ref), peak(grads_ref)
    for ref in (mine_ref, other_ref):
        ref[768:784, 0:128] = jnp.full((16, 128), acts_peak, F32).astype(BF16)
        ref[768:784, 128:384] = jnp.full((16, 256), grads_peak, F32).astype(BF16)


def arrange(core, grads, acts):
    vmem = pl.BlockSpec(memory_space=pltpu.VMEM)
    return pl.pallas_call(
        arrange_kernel,
        out_shape=[jax.ShapeDtypeStruct((784, TOK), BF16)] * 2,
        in_specs=[pl.BlockSpec(memory_space=pltpu.SMEM), vmem, vmem],
        out_specs=[vmem, vmem],
        compiler_params=pltpu.CompilerParams(vmem_limit_bytes=24 << 20),
    )(core.reshape(1), grads, acts)


def own_kernel(cols_ref, acts_ref, out_ref):
    for half in range(2):
        rows = slice(384 * half, 384 * (half + 1))
        out_ref[rows, :] = jnp.dot(cols_ref[rows, :], acts_ref[...], preferred_element_type=F32).astype(BF16)


def own_terms(cols, acts):
    return pl.pallas_call(
        own_kernel,
        grid=(4,),
        out_shape=jax.ShapeDtypeStruct((768, D), BF16),
        in_specs=[pl.BlockSpec((784, TOK), lambda i: (0, 0)), pl.BlockSpec((TOK, 768), lambda i: (0, i))],
        out_specs=pl.BlockSpec((768, 768), lambda i: (0, i)),
        compiler_params=pltpu.CompilerParams(vmem_limit_bytes=32 << 20),
        cost_estimate=pl.CostEstimate(flops=2 * 768 * TOK * D, bytes_accessed=8 << 20, transcendentals=0),
    )(cols, acts)


def pair_kernel(core_ref, mine_ref, their_ref, acts_ref, own_ref, out_ref, *, half):
    step = pl.program_id(0)
    core = core_ref[0]
    bound = jnp.zeros((16, 128), F32)
    for ref in (mine_ref, their_ref):
        bound = bound + TOK * ref[768:784, 0:128].astype(F32) * ref[768:784, 128:256].astype(F32)
    up = jnp.full((16, 128), 2.0 ** -14, F32)
    down = jnp.full((16, 128), 2.0 ** 14, F32)
    for k in range(-14, 14):
        over = bound > 2.0 ** (8 * k)
        up = jnp.where(over, up * 2.0, up)
        down = jnp.where(over, down * 0.5, down)
    scale = eighth(down[0:1, 0:1]) * 2.0 ** 15

    rows = slice(384 * half, 384 * (half + 1))
    term = jnp.dot(their_ref[rows, :], acts_ref[...], preferred_element_type=F32).astype(BF16)
    total = (own_ref[...].astype(F32) + term.astype(F32)) * scale
    for x in range(4):
        u = jnp.where(core == 0, x, step)
        v = jnp.where(core == 0, step, x)
        out_ref[u, pl.ds(pl.multiple_of(v * 96, 96), 96), :] = total[x * 96:(x + 1) * 96]

    if half == 1:
        @pl.when(step == 0)
        def _():
            for u in range(4):
                out_ref[u, 384:392, :] = jnp.broadcast_to(up[0:1, 0:1], (8, 768))
                out_ref[u, 392:400, :] = jnp.broadcast_to(down[0:1, 0:1], (8, 768))


def pair_sums(half, core, mine, theirs, acts, own):
    cols = pl.BlockSpec((784, TOK), lambda i: (0, 0))
    rows = 400 if half else 384
    return pl.pallas_call(
        functools.partial(pair_kernel, half=half),
        grid=(4,),
        out_shape=jax.ShapeDtypeStruct((4, rows, 768), F32),
        in_specs=[
            pl.BlockSpec(memory_space=pltpu.SMEM),
            cols,
            cols,
            pl.BlockSpec((TOK, 768), lambda i: (0, i)),
            pl.BlockSpec((384, 768), lambda i: (half, i)),
        ],
        out_specs=pl.BlockSpec((4, rows, 768), lambda i: (0, 0, 0)),
        compiler_params=pltpu.CompilerParams(vmem_limit_bytes=32 << 20),
        cost_estimate=pl.CostEstimate(flops=768 * TOK * D, bytes_accessed=9 << 20, transcendentals=0),
    )(core.reshape(1), mine, theirs, acts, own)


def scales(parts, rows):
    ups = [part[rows:rows + 1].astype(F32) for part in parts]
    downs = [part[rows + 8:rows + 9].astype(F32) for part in parts]
    return [eighth(up) for up in ups], functools.reduce(jnp.maximum, ups), functools.reduce(jnp.minimum, downs)


def add_parts(parts, factors, rows, top):
    return sum(part[:rows].astype(F32) * (factor * (1.0 / top)) for part, factor in zip(parts, factors))


def pack(ref, value):
    ref[0:48, :] = value[:, 0:128]
    ref[48:72, 0:64] = value[0:24, 128:192]
    ref[48:72, 64:128] = value[24:48, 128:192]


def unpack(ref, at, value):
    ref[at:at + 48, 0:128] = value[0:48]
    ref[at:at + 24, 128:192] = value[48:72, 0:64]
    ref[at + 24:at + 48, 128:192] = value[48:72, 64:128]


def z_kernel(tile_ref, up_ref, down_ref, out_ref):
    scale = eighth(down_ref[0:1, 0:1]) * 2.0 ** 11
    for zh in range(4):
        for zl in range(4):
            piece = tile_ref[zh * 48:(zh + 1) * 48, zl * 192:(zl + 1) * 192]
            pack(out_ref.at[zh * 4 + zl], piece * scale)
            out_ref[zh * 4 + zl, 72:80, :] = jnp.broadcast_to(up_ref[0:1, 0:1], (8, 128))


def z_pieces(tile, up, down):
    vmem = pl.BlockSpec(memory_space=pltpu.VMEM)
    return pl.pallas_call(
        z_kernel,
        out_shape=jax.ShapeDtypeStruct((16, 80, 128), F32),
        in_specs=[vmem, vmem, vmem],
        out_specs=vmem,
        compiler_params=pltpu.CompilerParams(vmem_limit_bytes=24 << 20),
    )(tile, up, down)


def square_kernel(grad_ref, out_ref):
    grad = grad_ref[...]
    out_ref[...] = jnp.full(out_ref.shape, jnp.sum(grad * grad), F32)


def sum_kernel(part_ref, out_ref):
    total = part_ref[0]
    for i in range(1, part_ref.shape[0]):
        total = total + part_ref[i]
    for i in range(out_ref.shape[0]):
        out_ref[i] = total


def to_send(kernel, count, value):
    vmem = pl.BlockSpec(memory_space=pltpu.VMEM)
    return pl.pallas_call(
        kernel, out_shape=jax.ShapeDtypeStruct((count, 1, 128), F32), in_specs=[vmem], out_specs=vmem
    )(value)


def update_kernel(square_ref, grad_ref, master_ref, first_ref, second_ref, *refs):
    new_master_ref, new_first_ref, new_second_ref, params_ref, tile_ref = refs
    square = square_ref[0]
    for i in range(1, 16):
        square = square + square_ref[i]
    rms = jnp.sqrt(square[:, 0:1] / (D * FO) + 1e-06)
    clip = jnp.minimum(1.0, 1.0 / rms)
    unpack(tile_ref, 0, grad_ref[...])
    clipped = clip * tile_ref[...]
    master = master_ref[...]
    new_first = 0.9 * first_ref[...] + 0.1 * clipped
    new_second = 0.95 * second_ref[...] + 0.05 * clipped * clipped
    new_master = master - 0.01 * (new_first / (jnp.sqrt(new_second) + 1e-08) + 0.1 * master)
    new_master_ref[...], new_first_ref[...], new_second_ref[...] = new_master, new_first, new_second
    for i in range(4):
        params_ref[i] = new_master.astype(BF16)


def update(square, grad, *state):
    vmem = pl.BlockSpec(memory_space=pltpu.VMEM)
    tile = jax.ShapeDtypeStruct((48, 192), F32)
    return pl.pallas_call(
        update_kernel,
        out_shape=[tile, tile, tile, jax.ShapeDtypeStruct((4, 48, 192), BF16)],
        in_specs=[vmem] * 5,
        out_specs=[vmem] * 4,
        scratch_shapes=[pltpu.VMEM((48, 192), F32)],
    )(square, grad, *state)


def cross_trade(value, first):
    groups = []
    for core in range(2):
        for a in range(4):
            fours = [(b, core, a) if core == first else (a, core, b) for b in range(4)]
            groups.append([(x * 2 + c) * 4 + y for x, c, y in fours])
    return lax.all_to_all(value, ("x", "c", "y"), 0, 0, axis_index_groups=groups, tiled=True)


def local(acts, grads, master, first, second):
    core = lax.axis_index("c")

    their_acts = swap(acts, "c")
    mine, other = arrange(core, grads, acts)
    their_cols = swap(other, "c")
    own = own_terms(mine, acts)
    halves = [pair_sums(half, core, mine, their_cols, their_acts, own) for half in range(2)]
    part = cross_trade(jnp.concatenate(halves, axis=1).astype(F16), 0)
    parts = [part[i] for i in range(4)]
    factors, up, down = scales(parts, 768)
    total = add_parts(parts, factors, 768, 2.0 ** 15) * (eighth(down) * 2.0 ** 13)
    send = [total[:384].reshape(4, 96, 768), total[384:].reshape(4, 96, 768)]
    send += [jnp.broadcast_to(row, (4, 8, 768)) for row in (up, down)]
    part = cross_trade(jnp.concatenate([part.astype(F16) for part in send], axis=1), 1)
    parts = [part[i] for i in range(4)]
    factors, up, down = scales(parts, 192)
    tile = add_parts(parts, factors, 192, 2.0 ** 13)

    part = trade(z_pieces(tile, up, down).astype(F16), ("zh", "zl"))
    ups = part[:, 72:73, 0:1].astype(F32)
    grad = jnp.sum(part[:, :72].astype(F32) * (eighth(ups) * 2.0 ** -11), axis=0)

    square = trade(to_send(square_kernel, 32, grad), ("x", "y", "c"))
    square = trade(to_send(sum_kernel, 16, square), ("zh", "zl"))
    *outs, params = update(square, grad, master.T, first.T, second.T)
    params = trade(params, "zh")
    params = trade(jnp.broadcast_to(params, (4, 4, 48, 192)), "x").reshape(16, 48, 192)
    theirs = swap(params, "c")
    params = jnp.where(core == 0, jnp.stack([params, theirs], 1), jnp.stack([theirs, params], 1))
    return (*[out.T for out in outs], params.reshape(FO, 192).T)


def solution(mesh):
    fine = Mesh(mesh.devices.reshape(4, 4, 2, 4, 4), ("x", "zh", "c", "y", "zl"))
    dp, seq = ("x", "zh", "c"), ("y", "zl")
    return jax.shard_map(
        local,
        mesh=fine,
        in_specs=(P(dp + seq, None), P(dp + seq, None), P(seq, dp), P(seq, dp), P(seq, dp)),
        out_specs=(P(seq, dp), P(seq, dp), P(seq, dp), P(seq, None)),
        check_vma=False,
    )
```

time: 185 us -> 176 us (0.951)
  other arithmetic: 9.43 us -> 5.06 us
  blocking collectives: 135 us -> 132 us
  local copies, waits for them, and re-layouts: 6.59 us -> 4.36 us
    convert_element_type x3 -> x1, other arithmetic: 5.39 us -> 0.02 us  [local(): part.astype(F16)]
    all_to_all x5, blocking collectives: 89 us -> 85.8 us  [trade(): return lax.all_to_all(value, axes, 0, 0, tiled=True)]
    pallas_call x2 -> x6, Pallas kernels: 8.07 us -> 9.73 us  [the longest x2 4.9 us: pair_sums(): pl.pallas_call(functools.partial(pair_kernel, half=half), grid=(4,), out_...]
    unnamed x13 -> x7, local copies, waits for them, and re-layouts: 4.03 us -> 4.01 us
where the time goes in v3:
time: 176 us; the launch traced here: 175 us
  blocking collectives  132 us (75%)
  starting transfers between devices  17.4 us (10%)
  Pallas kernels  14 us (8%)
  other arithmetic  5.06 us (3%)
  local copies, waits for them, and re-layouts  4.36 us (2%)
    all_to_all x5, blocking collectives, trade(): return lax.all_to_all(value, axes, 0, 0, tiled=True)  85.8 us
    all_to_all x2, blocking collectives, cross_trade(): lax.all_to_all(value, ('x', 'c', 'y'), 0, 0, axis_index_groups=groups, ti...  46.2 us
    ppermute x3, starting transfers between devices, swap(): return lax.ppermute(value, axis, [(0, 1), (1, 0)])  17.4 us
    pallas_call x2, Pallas kernels, pair_sums(): pl.pallas_call(functools.partial(pair_kernel, half=half), grid=(4,), out_...  4.9 us
    unnamed x7, local copies, waits for them, and re-layouts  4.01 us
    pallas_call x1, Pallas kernels, own_terms(): pl.pallas_call(own_kernel, grid=(4,), out_shape=jax.ShapeDtypeStruct((768...  3.59 us
  transfers between devices with their start and end apart: 3, of which 1 were waited for; matrix products, arithmetic and copies ran while one was open for 0% of the time, Pallas kernels for 2%

profile of v3, /device:TPU:1, one launch (start us, length us, event | category | flops | bytes accessed | tf_op | source)
XLA Modules:
  0.0 175.0 jit_solution(8792382372445012732)
XLA Ops:
  0.6 8.8 %collective-permute-start.1 = (bf16[384,3072]{1,0:T(8,128)(2,1)}, bf16[384,3072]{1,0:T(8,128)(2,1)S(1)}, u32[]{:S(2)}, u32[]{:S(2)}) collective-permute-start(bf16[384,3072]{1,0:T(8,128)(2,1)} %acts_ref.3), channel_id=1, source_target_pairs={{0,16},{16,0},{1,17},{17,1},{2,18},{18,2},{3,19},{19,3},{4,20},{20... | collective-permute-start | bytes 7077896 | tf_op jit(solution)/shard_map/ppermute | solution.py:19
  9.4 0.0 copy-start
  9.4 1.7 copy-done
  11.1 0.0 copy-start.2
  11.1 1.3 copy-done.2
  12.4 0.0 copy-start.1
  12.4 0.7 shard_map.84
  13.1 1.9 %collective-permute-start = (bf16[784,384]{1,0:T(8,128)(2,1)S(1)}, bf16[784,384]{1,0:T(8,128)(2,1)S(1)}, u32[]{:S(2)}, u32[]{:S(2)}) collective-permute-start(bf16[784,384]{1,0:T(8,128)(2,1)S(1)} %get-tuple-element.11), channel_id=1, source_target_pairs={{0,16},{16,0},{1,17},{17,1},{2,18},{18,2},{3,19},{19,3},{4,20},{20... | collective-permute-start | bytes 1806344 | tf_op jit(solution)/shard_map/ppermute | solution.py:19
  15.0 0.0 copy-done.1
  15.0 3.6 %shard_map.85.own_ref = bf16[768,3072]{1,0:T(8,128)(2,1)S(1)} custom-call(bf16[784,384]{1,0:T(8,128)(2,1)S(1)} %get-tuple-element.10.cols_ref.mine_ref, bf16[384,3072]{1,0:T(8,128)(2,1)S(1)} %copy-done.1), custom_call_target="tpu_custom_call" | custom-call | flops 1811939328 | bytes 8388608 | tf_op jit(solution)/shard_map/pallas_call | solution.py:79
  18.6 0.0 collective-permute-done.their_ref
  18.7 0.0 collective-permute-done.1.acts_ref
  18.7 2.4 %shard_map.86 = f32[4,384,768]{2,1,0:T(8,128)S(1)} custom-call(s32[1]{0:T(128)} %bitcast.core_ref, bf16[784,384]{1,0:T(8,128)(2,1)S(1)} %get-tuple-element.10.cols_ref.mine_ref, bf16[784,384]{1,0:T(8,128)(2,1)S(1)} %collective-permute-done.their_ref, bf16[384,3072]{1,0:T(8,128)(2,1)S(1)} %collective-permute-done.1.acts_ref, ...), custom_call_target="tpu_custom_call" | custom-call | flops 905969664 | bytes 9437184 | tf_op jit(solution)/shard_map/pallas_call | solution.py:123
  21.1 0.4 convert.21
  21.5 2.5 %shard_map.87 = f32[4,400,768]{2,1,0:T(8,128)S(1)} custom-call(s32[1]{0:T(128)} %bitcast.core_ref, bf16[784,384]{1,0:T(8,128)(2,1)S(1)} %get-tuple-element.10.cols_ref.mine_ref, bf16[784,384]{1,0:T(8,128)(2,1)S(1)} %collective-permute-done.their_ref, bf16[384,3072]{1,0:T(8,128)(2,1)S(1)} %collective-permute-done.1.acts_ref, ...), custom_call_target="tpu_custom_call" | custom-call | flops 905969664 | bytes 9437184 | tf_op jit(solution)/shard_map/pallas_call | solution.py:123
  23.9 0.4 convert.22
  24.3 1.2 pad_maximum_fusion
  25.5 32.5 %all_to_all.35 = f16[4,784,768]{2,1,0:T(8,128)(2,1)S(1)} all-to-all(f16[4,784,768]{2,1,0:T(8,128)(2,1)S(1)} %pad_maximum_fusion), channel_id=1, replica_groups={{0,128,256,384},{4,132,260,388},{8,136,264,392},{12,140,268,396},{16,20..., dimensions={0} | all-to-all | bytes 9633792 | tf_op jit(solution)/shard_map/all_to_all | solution.py:238
  58.1 0.1 multiply_reduce_fusion.9
  58.1 1.1 fusion.2
  59.2 0.2 fusion.21
  59.5 0.5 pad_maximum_fusion.1
  60.0 13.7 %all_to_all.36 = f16[4,208,768]{2,1,0:T(8,128)(2,1)S(1)} all-to-all(f16[4,208,768]{2,1,0:T(8,128)(2,1)S(1)} %pad_maximum_fusion.1), channel_id=1, replica_groups={{0,4,8,12},{128,132,136,140},{256,260,264,268},{384,388,392,396},{16,14..., dimensions={0} | all-to-all | bytes 2555904 | tf_op jit(solution)/shard_map/all_to_all | solution.py:238
  73.7 0.1 fusion.14
  73.7 0.2 fusion.5.tile_ref
  73.9 0.3 shard_map.88
  74.3 25.6 %all_to_all.37 = f16[16,80,128]{2,1,0:T(8,128)(2,1)S(1)} all-to-all(f16[16,80,128]{2,1,0:T(8,128)(2,1)S(1)} %convert_element_type.309), channel_id=1, replica_groups=mesh['x'=4,'zh'=4,'c'=2,'y'=4,'zl'=4] {'zh','zl'}, dimensions={0} | all-to-all | bytes 655360 | tf_op jit(solution)/shard_map/all_to_all | solution.py:23
  99.9 0.2 fusion.12
  100.1 0.7 multiply_reduce_fusion.grad_ref
  100.8 1.5 shard_map.89
  102.3 19.5 %all_to_all.38.part_ref = f32[32,1,128]{2,1,0:T(1,128)} all-to-all(f32[32,1,128]{2,1,0:T(1,128)} %shard_map.89), channel_id=1, replica_groups=mesh['x'=4,'zh'=4,'c'=2,'y'=4,'zl'=4] {'x','y','c'}, dimensions={0} | all-to-all | bytes 32768 | tf_op jit(solution)/shard_map/all_to_all | solution.py:23
  121.8 1.4 shard_map.90
  123.2 17.0 %all_to_all.39.square_ref = f32[16,1,128]{2,1,0:T(1,128)} all-to-all(f32[16,1,128]{2,1,0:T(1,128)} %shard_map.90), channel_id=1, replica_groups=mesh['x'=4,'zh'=4,'c'=2,'y'=4,'zl'=4] {'zh','zl'}, dimensions={0} | all-to-all | bytes 16384 | tf_op jit(solution)/shard_map/all_to_all | solution.py:23
  140.2 1.7 shard_map.91
  141.9 15.1 %all_to_all.40 = bf16[4,48,192]{2,1,0:T(8,128)(2,1)S(1)} all-to-all(bf16[4,48,192]{2,1,0:T(8,128)(2,1)} %get-tuple-element.15), channel_id=1, replica_groups=mesh['x'=4,'zh'=4,'c'=2,'y'=4,'zl'=4] {'zh'}, dimensions={0} | all-to-all | bytes 147456 | tf_op jit(solution)/shard_map/all_to_all | solution.py:23
  157.0 8.6 %all_to_all.41 = bf16[4,4,48,192]{3,2,1,0:T(8,128)(2,1)S(1)} all-to-all(bf16[4,4,48,192]{3,2,1,0:T(8,128)(2,1)S(1)} %broadcast_in_dim.15), channel_id=1, replica_groups=mesh['x'=4,'zh'=4,'c'=2,'y'=4,'zl'=4] {'x'}, dimensions={0} | all-to-all | bytes 589824 | tf_op jit(solution)/shard_map/all_to_all | solution.py:23
  165.6 6.7 %collective-permute-start.2 = (bf16[16,48,192]{2,1,0:T(8,128)(2,1)S(1)}, bf16[16,48,192]{2,1,0:T(8,128)(2,1)S(1)}, u32[]{:S(2)}, u32[]{:S(2)}) collective-permute-start(bf16[16,48,192]{2,1,0:T(8,128)(2,1)S(1)} %bitcast.62), channel_id=1, source_target_pairs={{0,16},{16,0},{1,17},{17,1},{2,18},{18,2},{3,19},{19,3},{4,20},{20... | collective-permute-start | bytes 884744 | tf_op jit(solution)/shard_map/ppermute | solution.py:19
  172.3 1.3 collective-permute-done.2
  173.6 0.2 maximum_select_fusion
  173.9 0.1 copy.12
  174.0 1.1 copy.13
  (6 shorter events, 0.1 us)
Async XLA Ops:
  0.6 18.0 %collective-permute-start.1 = (bf16[384,3072]{1,0:T(8,128)(2,1)}, bf16[384,3072]{1,0:T(8,128)(2,1)S(1)}, u32[]{:S(2)}, u32[]{:S(2)}) collective-permute-start(bf16[384,3072]{1,0:T(8,128)(2,1)} %acts_ref.3), channel_id=1, source_target_pairs={{0,16},{16,0},{1,17},{17,1},{2,18},{18,2},{3,19},{19,3},{4,20},{20... | collective-permute-start | bytes 7077896 | tf_op jit(solution)/shard_map/ppermute | solution.py:19
  9.4 1.7 copy-start
  11.1 1.3 copy-start.2
  12.4 2.7 %copy-start.1 = (bf16[384,3072]{1,0:T(8,128)(2,1)S(1)}, bf16[384,3072]{1,0:T(8,128)(2,1)}, u32[]{:S(2)}) copy-start(bf16[384,3072]{1,0:T(8,128)(2,1)} %acts_ref.3) | copy-start | bytes 7077892
  13.1 5.5 %collective-permute-start = (bf16[784,384]{1,0:T(8,128)(2,1)S(1)}, bf16[784,384]{1,0:T(8,128)(2,1)S(1)}, u32[]{:S(2)}, u32[]{:S(2)}) collective-permute-start(bf16[784,384]{1,0:T(8,128)(2,1)S(1)} %get-tuple-element.11), channel_id=1, source_target_pairs={{0,16},{16,0},{1,17},{17,1},{2,18},{18,2},{3,19},{19,3},{4,20},{20... | collective-permute-start | bytes 1806344 | tf_op jit(solution)/shard_map/ppermute | solution.py:19
  165.6 8.0 %collective-permute-start.2 = (bf16[16,48,192]{2,1,0:T(8,128)(2,1)S(1)}, bf16[16,48,192]{2,1,0:T(8,128)(2,1)S(1)}, u32[]{:S(2)}, u32[]{:S(2)}) collective-permute-start(bf16[16,48,192]{2,1,0:T(8,128)(2,1)S(1)} %bitcast.62), channel_id=1, source_target_pairs={{0,16},{16,0},{1,17},{17,1},{2,18},{18,2},{3,19},{19,3},{4,20},{20... | collective-permute-start | bytes 884744 | tf_op jit(solution)/shard_map/ppermute | solution.py:19

commit v4 on v3

--- a/solution.py
+++ b/solution.py
@@ -29,7 +29,14 @@
     return value * value
 
 
-def arrange_kernel(core_ref, grads_ref, acts_ref, mine_ref, other_ref):
+def peak(ref):
+    top = jnp.abs(ref[0:16, :])
+    for row in range(16, TOK, 16):
+        top = jnp.maximum(top, jnp.abs(ref[row:row + 16, :]))
+    return jnp.max(top.astype(F32))
+
+
+def arrange_kernel(core_ref, grads_ref, mine_ref, other_ref):
     def write(even_ref, odd_ref):
         for x in range(4):
             block = grads_ref[:, x * 384:(x + 1) * 384].T
@@ -46,95 +53,83 @@
     def _():
         write(other_ref, mine_ref)
 
-    def peak(ref):
-        top = jnp.abs(ref[0:16, :])
-        for row in range(16, TOK, 16):
-            top = jnp.maximum(top, jnp.abs(ref[row:row + 16, :]))
-        return jnp.max(top.astype(F32))
-
-    acts_peak, grads_peak = peak(acts_ref), peak(grads_ref)
-    for ref in (mine_ref, other_ref):
-        ref[768:784, 0:128] = jnp.full((16, 128), acts_peak, F32).astype(BF16)
-        ref[768:784, 128:384] = jnp.full((16, 256), grads_peak, F32).astype(BF16)
-
-
-def arrange(core, grads, acts):
+    top = jnp.full((16, TOK), peak(grads_ref), F32).astype(BF16)
+    mine_ref[768:784, :] = top
+    other_ref[768:784, :] = top
+
+
+def arrange(core, grads):
     vmem = pl.BlockSpec(memory_space=pltpu.VMEM)
     return pl.pallas_call(
         arrange_kernel,
         out_shape=[jax.ShapeDtypeStruct((784, TOK), BF16)] * 2,
-        in_specs=[pl.BlockSpec(memory_space=pltpu.SMEM), vmem, vmem],
+        in_specs=[pl.BlockSpec(memory_space=pltpu.SMEM), vmem],
         out_specs=[vmem, vmem],
-        compiler_params=pltpu.CompilerParams(vmem_limit_bytes=24 << 20),
-    )(core.reshape(1), grads, acts)
-
-
-def own_kernel(cols_ref, acts_ref, out_ref):
-    for half in range(2):
-        rows = slice(384 * half, 384 * (half + 1))
-        out_ref[rows, :] = jnp.dot(cols_ref[rows, :], acts_ref[...], preferred_element_type=F32).astype(BF16)
+        compiler_params=pltpu.CompilerParams(vmem_limit_bytes=8 << 20),
+    )(core.reshape(1), grads)
+
+
+def own_kernel(cols_ref, acts_ref, out_ref, peak_ref):
+    peak_ref[...] = jnp.full((8, 128), peak(acts_ref), F32)
+    for y in range(4):
+        lanes = slice(768 * y, 768 * (y + 1))
+        for half in range(2):
+            rows = slice(384 * half, 384 * (half + 1))
+            term = jnp.dot(cols_ref[rows, :], acts_ref[:, lanes], preferred_element_type=F32)
+            out_ref[rows, lanes] = term.astype(BF16)
 
 
 def own_terms(cols, acts):
+    vmem = pl.BlockSpec(memory_space=pltpu.VMEM)
     return pl.pallas_call(
         own_kernel,
-        grid=(4,),
-        out_shape=jax.ShapeDtypeStruct((768, D), BF16),
-        in_specs=[pl.BlockSpec((784, TOK), lambda i: (0, 0)), pl.BlockSpec((TOK, 768), lambda i: (0, i))],
-        out_specs=pl.BlockSpec((768, 768), lambda i: (0, i)),
-        compiler_params=pltpu.CompilerParams(vmem_limit_bytes=32 << 20),
+        out_shape=[jax.ShapeDtypeStruct((768, D), BF16), jax.ShapeDtypeStruct((8, 128), F32)],
+        in_specs=[vmem, vmem],
+        out_specs=[vmem, vmem],
+        compiler_params=pltpu.CompilerParams(vmem_limit_bytes=14 << 20),
         cost_estimate=pl.CostEstimate(flops=2 * 768 * TOK * D, bytes_accessed=8 << 20, transcendentals=0),
     )(cols, acts)
 
 
-def pair_kernel(core_ref, mine_ref, their_ref, acts_ref, own_ref, out_ref, *, half):
-    step = pl.program_id(0)
+def pair_kernel(core_ref, mine_ref, their_ref, acts_ref, own_ref, peak_ref, out_ref):
     core = core_ref[0]
-    bound = jnp.zeros((16, 128), F32)
-    for ref in (mine_ref, their_ref):
-        bound = bound + TOK * ref[768:784, 0:128].astype(F32) * ref[768:784, 128:256].astype(F32)
-    up = jnp.full((16, 128), 2.0 ** -14, F32)
-    down = jnp.full((16, 128), 2.0 ** 14, F32)
+    bound = peak_ref[...] * mine_ref[768:784, 0:128].astype(F32)[0:8]
+    bound = TOK * (bound + peak(acts_ref) * their_ref[768:784, 0:128].astype(F32)[0:8])
+    up = jnp.full((8, 128), 2.0 ** -14, F32)
+    down = jnp.full((8, 128), 2.0 ** 14, F32)
     for k in range(-14, 14):
         over = bound > 2.0 ** (8 * k)
         up = jnp.where(over, up * 2.0, up)
         down = jnp.where(over, down * 0.5, down)
     scale = eighth(down[0:1, 0:1]) * 2.0 ** 15
 
-    rows = slice(384 * half, 384 * (half + 1))
-    term = jnp.dot(their_ref[rows, :], acts_ref[...], preferred_element_type=F32).astype(BF16)
-    total = (own_ref[...].astype(F32) + term.astype(F32)) * scale
-    for x in range(4):
-        u = jnp.where(core == 0, x, step)
-        v = jnp.where(core == 0, step, x)
-        out_ref[u, pl.ds(pl.multiple_of(v * 96, 96), 96), :] = total[x * 96:(x + 1) * 96]
-
-    if half == 1:
-        @pl.when(step == 0)
-        def _():
-            for u in range(4):
-                out_ref[u, 384:392, :] = jnp.broadcast_to(up[0:1, 0:1], (8, 768))
-                out_ref[u, 392:400, :] = jnp.broadcast_to(down[0:1, 0:1], (8, 768))
-
-
-def pair_sums(half, core, mine, theirs, acts, own):
-    cols = pl.BlockSpec((784, TOK), lambda i: (0, 0))
-    rows = 400 if half else 384
-    return pl.pallas_call(
-        functools.partial(pair_kernel, half=half),
-        grid=(4,),
-        out_shape=jax.ShapeDtypeStruct((4, rows, 768), F32),
-        in_specs=[
-            pl.BlockSpec(memory_space=pltpu.SMEM),
-            cols,
-            cols,
-            pl.BlockSpec((TOK, 768), lambda i: (0, i)),
-            pl.BlockSpec((384, 768), lambda i: (half, i)),
-        ],
-        out_specs=pl.BlockSpec((4, rows, 768), lambda i: (0, 0, 0)),
-        compiler_params=pltpu.CompilerParams(vmem_limit_bytes=32 << 20),
-        cost_estimate=pl.CostEstimate(flops=768 * TOK * D, bytes_accessed=9 << 20, transcendentals=0),
-    )(core.reshape(1), mine, theirs, acts, own)
+    for half in range(2):
+        rows = slice(384 * half, 384 * (half + 1))
+        for y in range(4):
+            lanes = slice(768 * y, 768 * (y + 1))
+            term = jnp.dot(their_ref[rows, :], acts_ref[:, lanes], preferred_element_type=F32).astype(BF16)
+            total = (own_ref[rows, lanes].astype(F32) + term.astype(F32)) * scale
+            for x in range(4):
+                u = jnp.where(core == 0, x, y)
+                v = jnp.where(core == 0, y, x)
+                at = pl.multiple_of(half * 384 + v * 96, 96)
+                out_ref[u, pl.ds(at, 96), :] = total[x * 96:(x + 1) * 96]
+
+    for u in range(4):
+        out_ref[u, 768:776, :] = jnp.broadcast_to(up[0:1, 0:1], (8, 768))
+        out_ref[u, 776:784, :] = jnp.broadcast_to(down[0:1, 0:1], (8, 768))
+
+
+def pair_sums(core, mine, theirs, acts, own, own_peak):
+    vmem = pl.BlockSpec(memory_space=pltpu.VMEM)
+    return pl.pallas_call(
+        pair_kernel,
+        out_shape=jax.ShapeDtypeStruct((4, 784, 768), F32),
+        in_specs=[pl.BlockSpec(memory_space=pltpu.SMEM)] + [vmem] * 5,
+        out_specs=vmem,
+        compiler_params=pltpu.CompilerParams(vmem_limit_bytes=24 << 20),
+        cost_estimate=pl.CostEstimate(flops=2 * 768 * TOK * D, bytes_accessed=18 << 20, transcendentals=0),
+    )(core.reshape(1), mine, theirs, acts, own, own_peak)
 
 
 def scales(parts, rows):
@@ -175,7 +170,7 @@
         out_shape=jax.ShapeDtypeStruct((16, 80, 128), F32),
         in_specs=[vmem, vmem, vmem],
         out_specs=vmem,
-        compiler_params=pltpu.CompilerParams(vmem_limit_bytes=24 << 20),
+        compiler_params=pltpu.CompilerParams(vmem_limit_bytes=8 << 20),
     )(tile, up, down)
 
 
@@ -242,11 +237,11 @@
     core = lax.axis_index("c")
 
     their_acts = swap(acts, "c")
-    mine, other = arrange(core, grads, acts)
+    mine, other = arrange(core, grads)
     their_cols = swap(other, "c")
-    own = own_terms(mine, acts)
-    halves = [pair_sums(half, core, mine, their_cols, their_acts, own) for half in range(2)]
-    part = cross_trade(jnp.concatenate(halves, axis=1).astype(F16), 0)
+    own, own_peak = own_terms(mine, acts)
+    sums = pair_sums(core, mine, their_cols, their_acts, own, own_peak)
+    part = cross_trade(sums.astype(F16), 0)
     parts = [part[i] for i in range(4)]
     factors, up, down = scales(parts, 768)
     total = add_parts(parts, factors, 768, 2.0 ** 15) * (eighth(down) * 2.0 ** 13)

time: 176 us -> 172 us (0.977)
  Pallas kernels: 14 us -> 11.2 us
    pallas_call x3 -> x2, Pallas kernels: 8.5 us -> 5.82 us  [the longest x1 3.1 us: pair_sums(): pl.pallas_call(pair_kernel, out_shape=jax.ShapeDtypeStruct((4, 784, 768),...]
    unnamed x7 -> x5, local copies, waits for them, and re-layouts: 4.01 us -> 4 us
where the time goes in v4:
time: 172 us; the launch traced here: 171 us
  blocking collectives  132 us (77%)
  starting transfers between devices  17.4 us (10%)
  Pallas kernels  11.2 us (7%)
  local copies, waits for them, and re-layouts  4.36 us (3%)
  other arithmetic  3.74 us (2%)
    all_to_all x5, blocking collectives, trade(): return lax.all_to_all(value, axes, 0, 0, tiled=True)  85.8 us
    all_to_all x2, blocking collectives, cross_trade(): lax.all_to_all(value, ('x', 'c', 'y'), 0, 0, axis_index_groups=groups, ti...  46.2 us
    ppermute x3, starting transfers between devices, swap(): return lax.ppermute(value, axis, [(0, 1), (1, 0)])  17.4 us
    unnamed x5, local copies, waits for them, and re-layouts  4 us
  transfers between devices with their start and end apart: 3, of which 1 were waited for; matrix products, arithmetic and copies ran while one was open for 0% of the time, Pallas kernels for 2%

profile of v4, /device:TPU:1, one launch (start us, length us, event | category | flops | bytes accessed | tf_op | source)
XLA Modules:
  0.0 170.9 jit_solution(5306907219670548531)
XLA Ops:
  0.6 8.8 %collective-permute-start.1 = (bf16[384,3072]{1,0:T(8,128)(2,1)}, bf16[384,3072]{1,0:T(8,128)(2,1)S(1)}, u32[]{:S(2)}, u32[]{:S(2)}) collective-permute-start(bf16[384,3072]{1,0:T(8,128)(2,1)} %acts_ref.1), channel_id=1, source_target_pairs={{0,16},{16,0},{1,17},{17,1},{2,18},{18,2},{3,19},{19,3},{4,20},{20... | collective-permute-start | bytes 7077896 | tf_op jit(solution)/shard_map/ppermute | solution.py:19
  9.4 0.0 copy-start
  9.4 1.3 copy-done
  10.7 0.6 shard_map.84
  11.3 1.9 %collective-permute-start = (bf16[784,384]{1,0:T(8,128)(2,1)S(1)}, bf16[784,384]{1,0:T(8,128)(2,1)S(1)}, u32[]{:S(2)}, u32[]{:S(2)}) collective-permute-start(bf16[784,384]{1,0:T(8,128)(2,1)S(1)} %get-tuple-element.13), channel_id=1, source_target_pairs={{0,16},{16,0},{1,17},{17,1},{2,18},{18,2},{3,19},{19,3},{4,20},{20... | collective-permute-start | bytes 1806344 | tf_op jit(solution)/shard_map/ppermute | solution.py:19
  13.2 0.0 copy-start.1
  13.2 1.7 copy-done.1
  14.9 2.7 %shard_map.85 = (bf16[768,3072]{1,0:T(8,128)(2,1)S(1)}, f32[8,128]{1,0:T(8,128)S(1)}) custom-call(bf16[784,384]{1,0:T(8,128)(2,1)S(1)} %get-tuple-element.12.cols_ref.mine_ref, bf16[384,3072]{1,0:T(8,128)(2,1)S(1)} %copy-done.1), custom_call_target="tpu_custom_call" | custom-call | flops 1811939328 | bytes 8388608 | tf_op jit(solution)/shard_map/pallas_call | solution.py:84
  17.6 0.0 collective-permute-done.their_ref
  17.6 0.0 collective-permute-done.1.acts_ref
  17.6 3.1 %shard_map.86 = f32[4,784,768]{2,1,0:T(8,128)S(1)} custom-call(s32[1]{0:T(128)} %bitcast.core_ref, bf16[784,384]{1,0:T(8,128)(2,1)S(1)} %get-tuple-element.12.cols_ref.mine_ref, bf16[784,384]{1,0:T(8,128)(2,1)S(1)} %collective-permute-done.their_ref, bf16[384,3072]{1,0:T(8,128)(2,1)S(1)} %collective-permute-done.1.acts_ref, ...), custom_call_target="tpu_custom_call" | custom-call | flops 1811939328 | bytes 18874368 | tf_op jit(solution)/shard_map/pallas_call | solution.py:125
  20.7 0.6 convert_element_type.276
  21.3 32.5 %all_to_all.35 = f16[4,784,768]{2,1,0:T(8,128)(2,1)S(1)} all-to-all(f16[4,784,768]{2,1,0:T(8,128)(2,1)S(1)} %convert_element_type.276), channel_id=1, replica_groups={{0,128,256,384},{4,132,260,388},{8,136,264,392},{12,140,268,396},{16,20..., dimensions={0} | all-to-all | bytes 9633792 | tf_op jit(solution)/shard_map/all_to_all | solution.py:233
  53.9 0.1 multiply_reduce_fusion.9
  53.9 1.1 fusion.2
  55.0 0.2 fusion.21
  55.3 0.5 pad_maximum_fusion
  55.8 13.7 %all_to_all.36 = f16[4,208,768]{2,1,0:T(8,128)(2,1)S(1)} all-to-all(f16[4,208,768]{2,1,0:T(8,128)(2,1)S(1)} %pad_maximum_fusion), channel_id=1, replica_groups={{0,4,8,12},{128,132,136,140},{256,260,264,268},{384,388,392,396},{16,14..., dimensions={0} | all-to-all | bytes 2555904 | tf_op jit(solution)/shard_map/all_to_all | solution.py:233
  69.5 0.1 fusion.14
  69.5 0.2 fusion.5.tile_ref
  69.8 0.3 shard_map.87
  70.1 25.6 %all_to_all.37 = f16[16,80,128]{2,1,0:T(8,128)(2,1)S(1)} all-to-all(f16[16,80,128]{2,1,0:T(8,128)(2,1)S(1)} %convert_element_type.312), channel_id=1, replica_groups=mesh['x'=4,'zh'=4,'c'=2,'y'=4,'zl'=4] {'zh','zl'}, dimensions={0} | all-to-all | bytes 655360 | tf_op jit(solution)/shard_map/all_to_all | solution.py:23
  95.7 0.2 fusion.12
  95.9 0.7 multiply_reduce_fusion.grad_ref
  96.6 1.5 shard_map.88
  98.2 19.5 %all_to_all.38.part_ref = f32[32,1,128]{2,1,0:T(1,128)} all-to-all(f32[32,1,128]{2,1,0:T(1,128)} %shard_map.88), channel_id=1, replica_groups=mesh['x'=4,'zh'=4,'c'=2,'y'=4,'zl'=4] {'x','y','c'}, dimensions={0} | all-to-all | bytes 32768 | tf_op jit(solution)/shard_map/all_to_all | solution.py:23
  117.6 1.4 shard_map.89
  119.0 17.0 %all_to_all.39.square_ref = f32[16,1,128]{2,1,0:T(1,128)} all-to-all(f32[16,1,128]{2,1,0:T(1,128)} %shard_map.89), channel_id=1, replica_groups=mesh['x'=4,'zh'=4,'c'=2,'y'=4,'zl'=4] {'zh','zl'}, dimensions={0} | all-to-all | bytes 16384 | tf_op jit(solution)/shard_map/all_to_all | solution.py:23
  136.0 1.7 shard_map.90
  137.7 15.1 %all_to_all.40 = bf16[4,48,192]{2,1,0:T(8,128)(2,1)S(1)} all-to-all(bf16[4,48,192]{2,1,0:T(8,128)(2,1)} %get-tuple-element.19), channel_id=1, replica_groups=mesh['x'=4,'zh'=4,'c'=2,'y'=4,'zl'=4] {'zh'}, dimensions={0} | all-to-all | bytes 147456 | tf_op jit(solution)/shard_map/all_to_all | solution.py:23
  152.8 8.6 %all_to_all.41 = bf16[4,4,48,192]{3,2,1,0:T(8,128)(2,1)S(1)} all-to-all(bf16[4,4,48,192]{3,2,1,0:T(8,128)(2,1)S(1)} %broadcast_in_dim.15), channel_id=1, replica_groups=mesh['x'=4,'zh'=4,'c'=2,'y'=4,'zl'=4] {'x'}, dimensions={0} | all-to-all | bytes 589824 | tf_op jit(solution)/shard_map/all_to_all | solution.py:23
  161.5 6.7 %collective-permute-start.2 = (bf16[16,48,192]{2,1,0:T(8,128)(2,1)S(1)}, bf16[16,48,192]{2,1,0:T(8,128)(2,1)S(1)}, u32[]{:S(2)}, u32[]{:S(2)}) collective-permute-start(bf16[16,48,192]{2,1,0:T(8,128)(2,1)S(1)} %bitcast.62), channel_id=1, source_target_pairs={{0,16},{16,0},{1,17},{17,1},{2,18},{18,2},{3,19},{19,3},{4,20},{20... | collective-permute-start | bytes 884744 | tf_op jit(solution)/shard_map/ppermute | solution.py:19
  168.1 1.3 collective-permute-done.2
  169.5 0.2 maximum_select_fusion
  169.7 0.1 copy.12
  169.8 1.1 copy.13
  (6 shorter events, 0.1 us)
Async XLA Ops:
  0.6 17.0 %collective-permute-start.1 = (bf16[384,3072]{1,0:T(8,128)(2,1)}, bf16[384,3072]{1,0:T(8,128)(2,1)S(1)}, u32[]{:S(2)}, u32[]{:S(2)}) collective-permute-start(bf16[384,3072]{1,0:T(8,128)(2,1)} %acts_ref.1), channel_id=1, source_target_pairs={{0,16},{16,0},{1,17},{17,1},{2,18},{18,2},{3,19},{19,3},{4,20},{20... | collective-permute-start | bytes 7077896 | tf_op jit(solution)/shard_map/ppermute | solution.py:19
  9.4 1.3 copy-start
  11.3 6.3 %collective-permute-start = (bf16[784,384]{1,0:T(8,128)(2,1)S(1)}, bf16[784,384]{1,0:T(8,128)(2,1)S(1)}, u32[]{:S(2)}, u32[]{:S(2)}) collective-permute-start(bf16[784,384]{1,0:T(8,128)(2,1)S(1)} %get-tuple-element.13), channel_id=1, source_target_pairs={{0,16},{16,0},{1,17},{17,1},{2,18},{18,2},{3,19},{19,3},{4,20},{20... | collective-permute-start | bytes 1806344 | tf_op jit(solution)/shard_map/ppermute | solution.py:19
  13.2 1.7 copy-start.1
  161.5 8.0 %collective-permute-start.2 = (bf16[16,48,192]{2,1,0:T(8,128)(2,1)S(1)}, bf16[16,48,192]{2,1,0:T(8,128)(2,1)S(1)}, u32[]{:S(2)}, u32[]{:S(2)}) collective-permute-start(bf16[16,48,192]{2,1,0:T(8,128)(2,1)S(1)} %bitcast.62), channel_id=1, source_target_pairs={{0,16},{16,0},{1,17},{17,1},{2,18},{18,2},{3,19},{19,3},{4,20},{20... | collective-permute-start | bytes 884744 | tf_op jit(solution)/shard_map/ppermute | solution.py:19

commit v5 on v4

--- a/solution.py
+++ b/solution.py
@@ -36,35 +36,32 @@
     return jnp.max(top.astype(F32))
 
 
-def arrange_kernel(core_ref, grads_ref, mine_ref, other_ref):
-    def write(even_ref, odd_ref):
+def arrange_kernel(core_ref, grads_ref, out_ref):
+    def write(core):
         for x in range(4):
             block = grads_ref[:, x * 384:(x + 1) * 384].T
             for zh in range(4):
-                to = (zh // 2) * 384 + x * 96 + (zh % 2) * 48
-                even_ref[to:to + 48, :] = block[zh * 96:zh * 96 + 48]
-                odd_ref[to:to + 48, :] = block[zh * 96 + 48:zh * 96 + 96]
+                to, at = (zh // 2) * 384 + x * 96 + (zh % 2) * 48, zh * 96 + core * 48
+                out_ref[to:to + 48, :] = block[at:at + 48]
 
     @pl.when(core_ref[0] == 0)
     def _():
-        write(mine_ref, other_ref)
+        write(0)
 
     @pl.when(core_ref[0] != 0)
     def _():
-        write(other_ref, mine_ref)
-
-    top = jnp.full((16, TOK), peak(grads_ref), F32).astype(BF16)
-    mine_ref[768:784, :] = top
-    other_ref[768:784, :] = top
+        write(1)
+
+    out_ref[768:784, :] = jnp.full((16, TOK), peak(grads_ref), F32).astype(BF16)
 
 
 def arrange(core, grads):
     vmem = pl.BlockSpec(memory_space=pltpu.VMEM)
     return pl.pallas_call(
         arrange_kernel,
-        out_shape=[jax.ShapeDtypeStruct((784, TOK), BF16)] * 2,
+        out_shape=jax.ShapeDtypeStruct((784, TOK), BF16),
         in_specs=[pl.BlockSpec(memory_space=pltpu.SMEM), vmem],
-        out_specs=[vmem, vmem],
+        out_specs=vmem,
         compiler_params=pltpu.CompilerParams(vmem_limit_bytes=8 << 20),
     )(core.reshape(1), grads)
 
@@ -190,7 +187,11 @@
 def to_send(kernel, count, value):
     vmem = pl.BlockSpec(memory_space=pltpu.VMEM)
     return pl.pallas_call(
-        kernel, out_shape=jax.ShapeDtypeStruct((count, 1, 128), F32), in_specs=[vmem], out_specs=vmem
+        kernel,
+        out_shape=jax.ShapeDtypeStruct((count, 1, 128), F32),
+        in_specs=[vmem],
+        out_specs=vmem,
+        compiler_params=pltpu.CompilerParams(vmem_limit_bytes=1 << 20),
     )(value)
 
 
@@ -221,6 +222,7 @@
         in_specs=[vmem] * 5,
         out_specs=[vmem] * 4,
         scratch_shapes=[pltpu.VMEM((48, 192), F32)],
+        compiler_params=pltpu.CompilerParams(vmem_limit_bytes=2 << 20),
     )(square, grad, *state)
 
 
@@ -237,8 +239,8 @@
     core = lax.axis_index("c")
 
     their_acts = swap(acts, "c")
-    mine, other = arrange(core, grads)
-    their_cols = swap(other, "c")
+    their_cols = arrange(core, swap(grads, "c"))
+    mine = arrange(core, grads)
     own, own_peak = own_terms(mine, acts)
     sums = pair_sums(core, mine, their_cols, their_acts, own, own_peak)
     part = cross_trade(sums.astype(F16), 0)

time: 172 us -> 166 us (0.965)
  Pallas kernels: 11.2 us -> 8.17 us
  blocking collectives: 132 us -> 130 us
    pallas_call x2, Pallas kernels: 2.86 us -> 0.17 us  [to_send(): pl.pallas_call(kernel, out_shape=jax.ShapeDtypeStruct((count, 1, 128), F3...]
    all_to_all x5, blocking collectives: 85.8 us -> 83.8 us  [trade(): return lax.all_to_all(value, axes, 0, 0, tiled=True)]
    unnamed x5 -> x11, local copies, waits for them, and re-layouts: 4 us -> 4.02 us
where the time goes in v5:
time: 166 us
  blocking collectives  130 us (78%)
  starting transfers between devices  17.9 us (11%)
  Pallas kernels  8.17 us (5%)
  local copies, waits for them, and re-layouts  4.38 us (3%)
  other arithmetic  3.14 us (2%)
    all_to_all x5, blocking collectives, trade(): return lax.all_to_all(value, axes, 0, 0, tiled=True)  83.8 us
    all_to_all x2, blocking collectives, cross_trade(): lax.all_to_all(value, ('x', 'c', 'y'), 0, 0, axis_index_groups=groups, ti...  46.2 us
    ppermute x3, starting transfers between devices, swap(): return lax.ppermute(value, axis, [(0, 1), (1, 0)])  17.9 us
    unnamed x11, local copies, waits for them, and re-layouts  4.02 us
  transfers between devices with their start and end apart: 3, of which 1 were waited for; matrix products, arithmetic and copies ran while one was open for 0% of the time, Pallas kernels for 2%

profile of v5, /device:TPU:1, one launch (start us, length us, event | category | flops | bytes accessed | tf_op | source)
XLA Modules:
  0.0 165.7 jit_solution(3500984387618879128)
XLA Ops:
  0.6 8.8 %collective-permute-start.1 = (bf16[384,3072]{1,0:T(8,128)(2,1)}, bf16[384,3072]{1,0:T(8,128)(2,1)S(1)}, u32[]{:S(2)}, u32[]{:S(2)}) collective-permute-start(bf16[384,3072]{1,0:T(8,128)(2,1)} %acts_ref.1), channel_id=1, source_target_pairs={{0,16},{16,0},{1,17},{17,1},{2,18},{18,2},{3,19},{19,3},{4,20},{20... | collective-permute-start | bytes 7077896 | tf_op jit(solution)/shard_map/ppermute | solution.py:19
  9.4 1.9 %collective-permute-start = (bf16[384,1536]{1,0:T(8,128)(2,1)}, bf16[384,1536]{1,0:T(8,128)(2,1)S(1)}, u32[]{:S(2)}, u32[]{:S(2)}) collective-permute-start(bf16[384,1536]{1,0:T(8,128)(2,1)} %grads_ref.1), channel_id=1, source_target_pairs={{0,16},{16,0},{1,17},{17,1},{2,18},{18,2},{3,19},{19,3},{4,20},{20... | collective-permute-start | bytes 3538952 | tf_op jit(solution)/shard_map/ppermute | solution.py:19
  11.4 0.0 copy-start
  11.4 1.3 copy-done
  12.6 0.6 shard_map.84.cols_ref.mine_ref
  13.2 0.0 copy-start.4
  13.2 1.7 copy-done.4
  14.9 2.7 %shard_map.86 = (bf16[768,3072]{1,0:T(8,128)(2,1)S(1)}, f32[8,128]{1,0:T(8,128)S(1)}) custom-call(bf16[784,384]{1,0:T(8,128)(2,1)S(1)} %shard_map.84.cols_ref.mine_ref, bf16[384,3072]{1,0:T(8,128)(2,1)S(1)} %copy-done.4), custom_call_target="tpu_custom_call" | custom-call | flops 1811939328 | bytes 8388608 | tf_op jit(solution)/shard_map/pallas_call | solution.py:81
  17.6 0.0 collective-permute-done.grads_ref
  17.6 0.6 shard_map.85.their_ref
  18.2 0.0 collective-permute-done.1.acts_ref
  18.2 3.1 %shard_map.87 = f32[4,784,768]{2,1,0:T(8,128)S(1)} custom-call(s32[1]{0:T(128)} %bitcast.core_ref, bf16[784,384]{1,0:T(8,128)(2,1)S(1)} %shard_map.84.cols_ref.mine_ref, bf16[784,384]{1,0:T(8,128)(2,1)S(1)} %shard_map.85.their_ref, bf16[384,3072]{1,0:T(8,128)(2,1)S(1)} %collective-permute-done.1.acts_ref, bf16[768,3072]{1,0:T(8,128)(2,1)S(1)} %get-tuple-element.10.own_ref, ...), custom_call_target="tpu_custom_call" | custom-call | flops 1811939328 | bytes 18874368 | tf_op jit(solution)/shard_map/pallas_call | solution.py:122
  21.3 0.6 convert_element_type.276
  21.9 32.5 %all_to_all.35 = f16[4,784,768]{2,1,0:T(8,128)(2,1)S(1)} all-to-all(f16[4,784,768]{2,1,0:T(8,128)(2,1)S(1)} %convert_element_type.276), channel_id=1, replica_groups={{0,128,256,384},{4,132,260,388},{8,136,264,392},{12,140,268,396},{16,20..., dimensions={0} | all-to-all | bytes 9633792 | tf_op jit(solution)/shard_map/all_to_all | solution.py:235
  54.4 0.1 multiply_reduce_fusion.9
  54.5 1.1 fusion.2
  55.6 0.2 fusion.21
  55.9 0.5 pad_maximum_fusion
  56.4 13.7 %all_to_all.36 = f16[4,208,768]{2,1,0:T(8,128)(2,1)S(1)} all-to-all(f16[4,208,768]{2,1,0:T(8,128)(2,1)S(1)} %pad_maximum_fusion), channel_id=1, replica_groups={{0,4,8,12},{128,132,136,140},{256,260,264,268},{384,388,392,396},{16,14..., dimensions={0} | all-to-all | bytes 2555904 | tf_op jit(solution)/shard_map/all_to_all | solution.py:235
  70.0 0.1 fusion.14
  70.1 0.0 copy-start.1
  70.1 0.0 copy-start.2
  70.1 0.0 copy-start.3
  70.1 0.2 fusion.5.tile_ref
  70.4 0.3 shard_map.88
  70.7 25.6 %all_to_all.37 = f16[16,80,128]{2,1,0:T(8,128)(2,1)S(1)} all-to-all(f16[16,80,128]{2,1,0:T(8,128)(2,1)S(1)} %convert_element_type.312), channel_id=1, replica_groups=mesh['x'=4,'zh'=4,'c'=2,'y'=4,'zl'=4] {'zh','zl'}, dimensions={0} | all-to-all | bytes 655360 | tf_op jit(solution)/shard_map/all_to_all | solution.py:23
  96.3 0.2 fusion.12
  96.5 0.1 multiply_reduce_fusion.grad_ref
  96.7 0.1 shard_map.89
  96.8 18.3 %all_to_all.38.part_ref = f32[32,1,128]{2,1,0:T(1,128)S(1)} all-to-all(f32[32,1,128]{2,1,0:T(1,128)S(1)} %shard_map.89), channel_id=1, replica_groups=mesh['x'=4,'zh'=4,'c'=2,'y'=4,'zl'=4] {'x','y','c'}, dimensions={0} | all-to-all | bytes 32768 | tf_op jit(solution)/shard_map/all_to_all | solution.py:23
  115.1 16.9 %all_to_all.39.square_ref = f32[16,1,128]{2,1,0:T(1,128)S(1)} all-to-all(f32[16,1,128]{2,1,0:T(1,128)S(1)} %shard_map.90), channel_id=1, replica_groups=mesh['x'=4,'zh'=4,'c'=2,'y'=4,'zl'=4] {'zh','zl'}, dimensions={0} | all-to-all | bytes 16384 | tf_op jit(solution)/shard_map/all_to_all | solution.py:23
  132.0 0.0 copy-done.1
  132.0 0.0 copy-done.2
  132.0 0.0 copy-done.3
  132.1 0.8 shard_map.91
  132.8 14.3 %all_to_all.40 = bf16[4,48,192]{2,1,0:T(8,128)(2,1)S(1)} all-to-all(bf16[4,48,192]{2,1,0:T(8,128)(2,1)S(1)} %get-tuple-element.15), channel_id=1, replica_groups=mesh['x'=4,'zh'=4,'c'=2,'y'=4,'zl'=4] {'zh'}, dimensions={0} | all-to-all | bytes 147456 | tf_op jit(solution)/shard_map/all_to_all | solution.py:23
  147.2 8.6 %all_to_all.41 = bf16[4,4,48,192]{3,2,1,0:T(8,128)(2,1)S(1)} all-to-all(bf16[4,4,48,192]{3,2,1,0:T(8,128)(2,1)S(1)} %broadcast_in_dim.15), channel_id=1, replica_groups=mesh['x'=4,'zh'=4,'c'=2,'y'=4,'zl'=4] {'x'}, dimensions={0} | all-to-all | bytes 589824 | tf_op jit(solution)/shard_map/all_to_all | solution.py:23
  155.8 7.2 %collective-permute-start.2 = (bf16[16,48,192]{2,1,0:T(8,128)(2,1)S(1)}, bf16[16,48,192]{2,1,0:T(8,128)(2,1)S(1)}, u32[]{:S(2)}, u32[]{:S(2)}) collective-permute-start(bf16[16,48,192]{2,1,0:T(8,128)(2,1)S(1)} %bitcast.65), channel_id=1, source_target_pairs={{0,16},{16,0},{1,17},{17,1},{2,18},{18,2},{3,19},{19,3},{4,20},{20... | collective-permute-start | bytes 884744 | tf_op jit(solution)/shard_map/ppermute | solution.py:19
  163.0 1.3 collective-permute-done.2
  164.3 0.2 maximum_select_fusion
  164.6 0.1 copy.12
  164.7 1.1 copy.13
  (7 shorter events, 0.2 us)
Async XLA Ops:
  0.6 17.6 %collective-permute-start.1 = (bf16[384,3072]{1,0:T(8,128)(2,1)}, bf16[384,3072]{1,0:T(8,128)(2,1)S(1)}, u32[]{:S(2)}, u32[]{:S(2)}) collective-permute-start(bf16[384,3072]{1,0:T(8,128)(2,1)} %acts_ref.1), channel_id=1, source_target_pairs={{0,16},{16,0},{1,17},{17,1},{2,18},{18,2},{3,19},{19,3},{4,20},{20... | collective-permute-start | bytes 7077896 | tf_op jit(solution)/shard_map/ppermute | solution.py:19
  9.4 8.2 %collective-permute-start = (bf16[384,1536]{1,0:T(8,128)(2,1)}, bf16[384,1536]{1,0:T(8,128)(2,1)S(1)}, u32[]{:S(2)}, u32[]{:S(2)}) collective-permute-start(bf16[384,1536]{1,0:T(8,128)(2,1)} %grads_ref.1), channel_id=1, source_target_pairs={{0,16},{16,0},{1,17},{17,1},{2,18},{18,2},{3,19},{19,3},{4,20},{20... | collective-permute-start | bytes 3538952 | tf_op jit(solution)/shard_map/ppermute | solution.py:19
  11.4 1.3 copy-start
  13.2 1.7 %copy-start.4 = (bf16[384,3072]{1,0:T(8,128)(2,1)S(1)}, bf16[384,3072]{1,0:T(8,128)(2,1)}, u32[]{:S(2)}) copy-start(bf16[384,3072]{1,0:T(8,128)(2,1)} %acts_ref.1) | copy-start | bytes 7077892
  70.1 61.9 %copy-start.1 = (f32[192,48]{0,1:T(8,128)S(1)}, f32[192,48]{0,1:T(8,128)}, u32[]{:S(2)}) copy-start(f32[192,48]{0,1:T(8,128)} %param.7) | copy-start | bytes 110596
  70.1 61.9 %copy-start.2 = (f32[192,48]{0,1:T(8,128)S(1)}, f32[192,48]{0,1:T(8,128)}, u32[]{:S(2)}) copy-start(f32[192,48]{0,1:T(8,128)} %param.8) | copy-start | bytes 110596
  70.1 61.9 %copy-start.3 = (f32[192,48]{0,1:T(8,128)S(1)}, f32[192,48]{0,1:T(8,128)}, u32[]{:S(2)}) copy-start(f32[192,48]{0,1:T(8,128)} %param.9) | copy-start | bytes 110596
  155.8 8.5 %collective-permute-start.2 = (bf16[16,48,192]{2,1,0:T(8,128)(2,1)S(1)}, bf16[16,48,192]{2,1,0:T(8,128)(2,1)S(1)}, u32[]{:S(2)}, u32[]{:S(2)}) collective-permute-start(bf16[16,48,192]{2,1,0:T(8,128)(2,1)S(1)} %bitcast.65), channel_id=1, source_target_pairs={{0,16},{16,0},{1,17},{17,1},{2,18},{18,2},{3,19},{19,3},{4,20},{20... | collective-permute-start | bytes 884744 | tf_op jit(solution)/shard_map/ppermute | solution.py:19

commit v6 on v5

--- a/solution.py
+++ b/solution.py
@@ -114,14 +114,13 @@
 
     for u in range(4):
         out_ref[u, 768:776, :] = jnp.broadcast_to(up[0:1, 0:1], (8, 768))
-        out_ref[u, 776:784, :] = jnp.broadcast_to(down[0:1, 0:1], (8, 768))
 
 
 def pair_sums(core, mine, theirs, acts, own, own_peak):
     vmem = pl.BlockSpec(memory_space=pltpu.VMEM)
     return pl.pallas_call(
         pair_kernel,
-        out_shape=jax.ShapeDtypeStruct((4, 784, 768), F32),
+        out_shape=jax.ShapeDtypeStruct((4, 776, 768), F32),
         in_specs=[pl.BlockSpec(memory_space=pltpu.SMEM)] + [vmem] * 5,
         out_specs=vmem,
         compiler_params=pltpu.CompilerParams(vmem_limit_bytes=24 << 20),
@@ -131,8 +130,8 @@
 
 def scales(parts, rows):
     ups = [part[rows:rows + 1].astype(F32) for part in parts]
-    downs = [part[rows + 8:rows + 9].astype(F32) for part in parts]
-    return [eighth(up) for up in ups], functools.reduce(jnp.maximum, ups), functools.reduce(jnp.minimum, downs)
+    up = functools.reduce(jnp.maximum, ups)
+    return [eighth(one) for one in ups], up, 1.0 / up
 
 
 def add_parts(parts, factors, rows, top):
@@ -248,7 +247,7 @@
     factors, up, down = scales(parts, 768)
     total = add_parts(parts, factors, 768, 2.0 ** 15) * (eighth(down) * 2.0 ** 13)
     send = [total[:384].reshape(4, 96, 768), total[384:].reshape(4, 96, 768)]
-    send += [jnp.broadcast_to(row, (4, 8, 768)) for row in (up, down)]
+    send.append(jnp.broadcast_to(up, (4, 8, 768)))
     part = cross_trade(jnp.concatenate([part.astype(F16) for part in send], axis=1), 1)
     parts = [part[i] for i in range(4)]
     factors, up, down = scales(parts, 192)

time: 166 us -> 166 us (level)
  no operation moved by 1% of the time
where the time goes in v6:
time: 166 us; the launch traced here: 165 us
  blocking collectives  129 us (78%)
  starting transfers between devices  17.9 us (11%)
  Pallas kernels  8.17 us (5%)
  local copies, waits for them, and re-layouts  4.37 us (3%)
  other arithmetic  3 us (2%)
    all_to_all x5, blocking collectives, trade(): return lax.all_to_all(value, axes, 0, 0, tiled=True)  83.5 us
    all_to_all x2, blocking collectives, cross_trade(): lax.all_to_all(value, ('x', 'c', 'y'), 0, 0, axis_index_groups=groups, ti...  45.9 us
    ppermute x3, starting transfers between devices, swap(): return lax.ppermute(value, axis, [(0, 1), (1, 0)])  17.9 us
    unnamed x11, local copies, waits for them, and re-layouts  4.02 us
  transfers between devices with their start and end apart: 3, of which 1 were waited for; matrix products, arithmetic and copies ran while one was open for 0% of the time, Pallas kernels for 2%

profile of v6, /device:TPU:1, one launch (start us, length us, event | category | flops | bytes accessed | tf_op | source)
XLA Modules:
  0.0 165.1 jit_solution(13179398429454595598)
XLA Ops:
  0.6 8.8 %collective-permute-start.1 = (bf16[384,3072]{1,0:T(8,128)(2,1)}, bf16[384,3072]{1,0:T(8,128)(2,1)S(1)}, u32[]{:S(2)}, u32[]{:S(2)}) collective-permute-start(bf16[384,3072]{1,0:T(8,128)(2,1)} %acts_ref.1), channel_id=1, source_target_pairs={{0,16},{16,0},{1,17},{17,1},{2,18},{18,2},{3,19},{19,3},{4,20},{20... | collective-permute-start | bytes 7077896 | tf_op jit(solution)/shard_map/ppermute | solution.py:19
  9.4 1.9 %collective-permute-start = (bf16[384,1536]{1,0:T(8,128)(2,1)}, bf16[384,1536]{1,0:T(8,128)(2,1)S(1)}, u32[]{:S(2)}, u32[]{:S(2)}) collective-permute-start(bf16[384,1536]{1,0:T(8,128)(2,1)} %grads_ref.1), channel_id=1, source_target_pairs={{0,16},{16,0},{1,17},{17,1},{2,18},{18,2},{3,19},{19,3},{4,20},{20... | collective-permute-start | bytes 3538952 | tf_op jit(solution)/shard_map/ppermute | solution.py:19
  11.4 0.0 copy-start
  11.4 1.3 copy-done
  12.6 0.6 shard_map.84.cols_ref.mine_ref
  13.2 0.0 copy-start.4
  13.2 1.7 %copy-done.4 = bf16[384,3072]{1,0:T(8,128)(2,1)S(1)} copy-done((bf16[384,3072]{1,0:T(8,128)(2,1)S(1)}, bf16[384,3072]{1,0:T(8,128)(2,1)}, u32[]{:S(2)}) %copy-start.4) | copy-done | bytes 2359320
  14.9 2.7 %shard_map.86 = (bf16[768,3072]{1,0:T(8,128)(2,1)S(1)}, f32[8,128]{1,0:T(8,128)S(1)}) custom-call(bf16[784,384]{1,0:T(8,128)(2,1)S(1)} %shard_map.84.cols_ref.mine_ref, bf16[384,3072]{1,0:T(8,128)(2,1)S(1)} %copy-done.4), custom_call_target="tpu_custom_call" | custom-call | flops 1811939328 | bytes 8388608 | tf_op jit(solution)/shard_map/pallas_call | solution.py:81
  17.6 0.0 collective-permute-done.grads_ref
  17.6 0.6 shard_map.85.their_ref
  18.2 0.0 collective-permute-done.1.acts_ref
  18.2 3.1 %shard_map.87 = f32[4,776,768]{2,1,0:T(8,128)S(1)} custom-call(s32[1]{0:T(128)} %bitcast.core_ref, bf16[784,384]{1,0:T(8,128)(2,1)S(1)} %shard_map.84.cols_ref.mine_ref, bf16[784,384]{1,0:T(8,128)(2,1)S(1)} %shard_map.85.their_ref, bf16[384,3072]{1,0:T(8,128)(2,1)S(1)} %collective-permute-done.1.acts_ref, bf16[768,3072]{1,0:T(8,128)(2,1)S(1)} %get-tuple-element.10.own_ref, ...), custom_call_target="tpu_custom_call" | custom-call | flops 1811939328 | bytes 18874368 | tf_op jit(solution)/shard_map/pallas_call | solution.py:121
  21.3 0.6 convert_element_type.209
  21.9 32.5 %all_to_all.35 = f16[4,776,768]{2,1,0:T(8,128)(2,1)S(1)} all-to-all(f16[4,776,768]{2,1,0:T(8,128)(2,1)S(1)} %convert_element_type.209), channel_id=1, replica_groups={{0,128,256,384},{4,132,260,388},{8,136,264,392},{12,140,268,396},{16,20..., dimensions={0} | all-to-all | bytes 9535488 | tf_op jit(solution)/shard_map/all_to_all | solution.py:234
  54.4 0.1 multiply_reduce_fusion.8
  54.5 1.1 fusion.2
  55.5 0.2 fusion.17
  55.8 0.4 pad_maximum_fusion
  56.2 13.4 %all_to_all.36 = f16[4,200,768]{2,1,0:T(8,128)(2,1)S(1)} all-to-all(f16[4,200,768]{2,1,0:T(8,128)(2,1)S(1)} %pad_maximum_fusion), channel_id=1, replica_groups={{0,4,8,12},{128,132,136,140},{256,260,264,268},{384,388,392,396},{16,14..., dimensions={0} | all-to-all | bytes 2457600 | tf_op jit(solution)/shard_map/all_to_all | solution.py:234
  69.7 0.0 copy-start.1
  69.7 0.0 copy-start.2
  69.7 0.0 copy-start.3
  69.7 0.2 fusion.5.tile_ref
  69.9 0.3 shard_map.88
  70.3 25.4 %all_to_all.37 = f16[16,80,128]{2,1,0:T(8,128)(2,1)S(1)} all-to-all(f16[16,80,128]{2,1,0:T(8,128)(2,1)S(1)} %convert_element_type.237), channel_id=1, replica_groups=mesh['x'=4,'zh'=4,'c'=2,'y'=4,'zl'=4] {'zh','zl'}, dimensions={0} | all-to-all | bytes 655360 | tf_op jit(solution)/shard_map/all_to_all | solution.py:23
  95.6 0.2 fusion.12
  95.9 0.1 multiply_reduce_fusion.grad_ref
  96.0 0.1 shard_map.89
  96.1 18.3 %all_to_all.38.part_ref = f32[32,1,128]{2,1,0:T(1,128)S(1)} all-to-all(f32[32,1,128]{2,1,0:T(1,128)S(1)} %shard_map.89), channel_id=1, replica_groups=mesh['x'=4,'zh'=4,'c'=2,'y'=4,'zl'=4] {'x','y','c'}, dimensions={0} | all-to-all | bytes 32768 | tf_op jit(solution)/shard_map/all_to_all | solution.py:23
  114.4 17.0 %all_to_all.39.square_ref = f32[16,1,128]{2,1,0:T(1,128)S(1)} all-to-all(f32[16,1,128]{2,1,0:T(1,128)S(1)} %shard_map.90), channel_id=1, replica_groups=mesh['x'=4,'zh'=4,'c'=2,'y'=4,'zl'=4] {'zh','zl'}, dimensions={0} | all-to-all | bytes 16384 | tf_op jit(solution)/shard_map/all_to_all | solution.py:23
  131.4 0.0 copy-done.1
  131.4 0.0 copy-done.2
  131.4 0.0 copy-done.3
  131.4 0.8 shard_map.91
  132.2 14.3 %all_to_all.40 = bf16[4,48,192]{2,1,0:T(8,128)(2,1)S(1)} all-to-all(bf16[4,48,192]{2,1,0:T(8,128)(2,1)S(1)} %get-tuple-element.15), channel_id=1, replica_groups=mesh['x'=4,'zh'=4,'c'=2,'y'=4,'zl'=4] {'zh'}, dimensions={0} | all-to-all | bytes 147456 | tf_op jit(solution)/shard_map/all_to_all | solution.py:23
  146.5 8.6 %all_to_all.41 = bf16[4,4,48,192]{3,2,1,0:T(8,128)(2,1)S(1)} all-to-all(bf16[4,4,48,192]{3,2,1,0:T(8,128)(2,1)S(1)} %broadcast_in_dim.9), channel_id=1, replica_groups=mesh['x'=4,'zh'=4,'c'=2,'y'=4,'zl'=4] {'x'}, dimensions={0} | all-to-all | bytes 589824 | tf_op jit(solution)/shard_map/all_to_all | solution.py:23
  155.1 7.2 %collective-permute-start.2 = (bf16[16,48,192]{2,1,0:T(8,128)(2,1)S(1)}, bf16[16,48,192]{2,1,0:T(8,128)(2,1)S(1)}, u32[]{:S(2)}, u32[]{:S(2)}) collective-permute-start(bf16[16,48,192]{2,1,0:T(8,128)(2,1)S(1)} %bitcast.64), channel_id=1, source_target_pairs={{0,16},{16,0},{1,17},{17,1},{2,18},{18,2},{3,19},{19,3},{4,20},{20... | collective-permute-start | bytes 884744 | tf_op jit(solution)/shard_map/ppermute | solution.py:19
  162.3 1.3 collective-permute-done.2
  163.7 0.2 maximum_select_fusion
  163.9 0.1 copy.12
  164.0 1.1 copy.13
  (7 shorter events, 0.2 us)
Async XLA Ops:
  0.6 17.6 %collective-permute-start.1 = (bf16[384,3072]{1,0:T(8,128)(2,1)}, bf16[384,3072]{1,0:T(8,128)(2,1)S(1)}, u32[]{:S(2)}, u32[]{:S(2)}) collective-permute-start(bf16[384,3072]{1,0:T(8,128)(2,1)} %acts_ref.1), channel_id=1, source_target_pairs={{0,16},{16,0},{1,17},{17,1},{2,18},{18,2},{3,19},{19,3},{4,20},{20... | collective-permute-start | bytes 7077896 | tf_op jit(solution)/shard_map/ppermute | solution.py:19
  9.4 8.2 %collective-permute-start = (bf16[384,1536]{1,0:T(8,128)(2,1)}, bf16[384,1536]{1,0:T(8,128)(2,1)S(1)}, u32[]{:S(2)}, u32[]{:S(2)}) collective-permute-start(bf16[384,1536]{1,0:T(8,128)(2,1)} %grads_ref.1), channel_id=1, source_target_pairs={{0,16},{16,0},{1,17},{17,1},{2,18},{18,2},{3,19},{19,3},{4,20},{20... | collective-permute-start | bytes 3538952 | tf_op jit(solution)/shard_map/ppermute | solution.py:19
  11.4 1.3 copy-start
  13.2 1.7 %copy-start.4 = (bf16[384,3072]{1,0:T(8,128)(2,1)S(1)}, bf16[384,3072]{1,0:T(8,128)(2,1)}, u32[]{:S(2)}) copy-start(bf16[384,3072]{1,0:T(8,128)(2,1)} %acts_ref.1) | copy-start | bytes 7077892
  69.7 61.7 %copy-start.1 = (f32[192,48]{0,1:T(8,128)S(1)}, f32[192,48]{0,1:T(8,128)}, u32[]{:S(2)}) copy-start(f32[192,48]{0,1:T(8,128)} %param.7) | copy-start | bytes 110596
  69.7 61.7 %copy-start.2 = (f32[192,48]{0,1:T(8,128)S(1)}, f32[192,48]{0,1:T(8,128)}, u32[]{:S(2)}) copy-start(f32[192,48]{0,1:T(8,128)} %param.8) | copy-start | bytes 110596
  69.7 61.7 %copy-start.3 = (f32[192,48]{0,1:T(8,128)S(1)}, f32[192,48]{0,1:T(8,128)}, u32[]{:S(2)}) copy-start(f32[192,48]{0,1:T(8,128)} %param.9) | copy-start | bytes 110596
  155.1 8.5 %collective-permute-start.2 = (bf16[16,48,192]{2,1,0:T(8,128)(2,1)S(1)}, bf16[16,48,192]{2,1,0:T(8,128)(2,1)S(1)}, u32[]{:S(2)}, u32[]{:S(2)}) collective-permute-start(bf16[16,48,192]{2,1,0:T(8,128)(2,1)S(1)} %bitcast.64), channel_id=1, source_target_pairs={{0,16},{16,0},{1,17},{17,1},{2,18},{18,2},{3,19},{19,3},{4,20},{20... | collective-permute-start | bytes 884744 | tf_op jit(solution)/shard_map/ppermute | solution.py:19

commit v7 on v6

--- a/solution.py
+++ b/solution.py
@@ -70,10 +70,8 @@
     peak_ref[...] = jnp.full((8, 128), peak(acts_ref), F32)
     for y in range(4):
         lanes = slice(768 * y, 768 * (y + 1))
-        for half in range(2):
-            rows = slice(384 * half, 384 * (half + 1))
-            term = jnp.dot(cols_ref[rows, :], acts_ref[:, lanes], preferred_element_type=F32)
-            out_ref[rows, lanes] = term.astype(BF16)
+        term = jnp.dot(cols_ref[0:768, :], acts_ref[:, lanes], preferred_element_type=F32)
+        out_ref[:, lanes] = term.astype(BF16)
 
 
 def own_terms(cols, acts):

time: 166 us -> 166 us (level)
  no operation moved by 1% of the time
where the time goes in v7:
time: 166 us; the launch traced here: 165 us
  blocking collectives  129 us (78%)
  starting transfers between devices  17.9 us (11%)
  Pallas kernels  8.13 us (5%)
  local copies, waits for them, and re-layouts  4.37 us (3%)
  other arithmetic  3 us (2%)
    all_to_all x5, blocking collectives, trade(): return lax.all_to_all(value, axes, 0, 0, tiled=True)  83.5 us
    all_to_all x2, blocking collectives, cross_trade(): lax.all_to_all(value, ('x', 'c', 'y'), 0, 0, axis_index_groups=groups, ti...  45.9 us
    ppermute x3, starting transfers between devices, swap(): return lax.ppermute(value, axis, [(0, 1), (1, 0)])  17.9 us
    unnamed x11, local copies, waits for them, and re-layouts  4.02 us
  transfers between devices with their start and end apart: 3, of which 1 were waited for; matrix products, arithmetic and copies ran while one was open for 0% of the time, Pallas kernels for 2%

profile of v7, /device:TPU:1, one launch (start us, length us, event | category | flops | bytes accessed | tf_op | source)
XLA Modules:
  0.0 165.0 jit_solution(189269932163853592)
XLA Ops:
  0.6 8.8 %collective-permute-start.1 = (bf16[384,3072]{1,0:T(8,128)(2,1)}, bf16[384,3072]{1,0:T(8,128)(2,1)S(1)}, u32[]{:S(2)}, u32[]{:S(2)}) collective-permute-start(bf16[384,3072]{1,0:T(8,128)(2,1)} %acts_ref.1), channel_id=1, source_target_pairs={{0,16},{16,0},{1,17},{17,1},{2,18},{18,2},{3,19},{19,3},{4,20},{20... | collective-permute-start | bytes 7077896 | tf_op jit(solution)/shard_map/ppermute | solution.py:19
  9.4 1.9 %collective-permute-start = (bf16[384,1536]{1,0:T(8,128)(2,1)}, bf16[384,1536]{1,0:T(8,128)(2,1)S(1)}, u32[]{:S(2)}, u32[]{:S(2)}) collective-permute-start(bf16[384,1536]{1,0:T(8,128)(2,1)} %grads_ref.1), channel_id=1, source_target_pairs={{0,16},{16,0},{1,17},{17,1},{2,18},{18,2},{3,19},{19,3},{4,20},{20... | collective-permute-start | bytes 3538952 | tf_op jit(solution)/shard_map/ppermute | solution.py:19
  11.4 0.0 copy-start
  11.4 1.3 copy-done
  12.6 0.6 shard_map.84.cols_ref.mine_ref
  13.2 0.0 copy-start.4
  13.2 1.7 %copy-done.4 = bf16[384,3072]{1,0:T(8,128)(2,1)S(1)} copy-done((bf16[384,3072]{1,0:T(8,128)(2,1)S(1)}, bf16[384,3072]{1,0:T(8,128)(2,1)}, u32[]{:S(2)}) %copy-start.4) | copy-done | bytes 2359320
  14.9 2.7 %shard_map.86 = (bf16[768,3072]{1,0:T(8,128)(2,1)S(1)}, f32[8,128]{1,0:T(8,128)S(1)}) custom-call(bf16[784,384]{1,0:T(8,128)(2,1)S(1)} %shard_map.84.cols_ref.mine_ref, bf16[384,3072]{1,0:T(8,128)(2,1)S(1)} %copy-done.4), custom_call_target="tpu_custom_call" | custom-call | flops 1811939328 | bytes 8388608 | tf_op jit(solution)/shard_map/pallas_call | solution.py:79
  17.6 0.0 collective-permute-done.grads_ref
  17.6 0.6 shard_map.85.their_ref
  18.1 0.0 collective-permute-done.1.acts_ref
  18.2 3.1 %shard_map.87 = f32[4,776,768]{2,1,0:T(8,128)S(1)} custom-call(s32[1]{0:T(128)} %bitcast.core_ref, bf16[784,384]{1,0:T(8,128)(2,1)S(1)} %shard_map.84.cols_ref.mine_ref, bf16[784,384]{1,0:T(8,128)(2,1)S(1)} %shard_map.85.their_ref, bf16[384,3072]{1,0:T(8,128)(2,1)S(1)} %collective-permute-done.1.acts_ref, bf16[768,3072]{1,0:T(8,128)(2,1)S(1)} %get-tuple-element.10.own_ref, ...), custom_call_target="tpu_custom_call" | custom-call | flops 1811939328 | bytes 18874368 | tf_op jit(solution)/shard_map/pallas_call | solution.py:119
  21.3 0.6 convert_element_type.209
  21.9 32.5 %all_to_all.35 = f16[4,776,768]{2,1,0:T(8,128)(2,1)S(1)} all-to-all(f16[4,776,768]{2,1,0:T(8,128)(2,1)S(1)} %convert_element_type.209), channel_id=1, replica_groups={{0,128,256,384},{4,132,260,388},{8,136,264,392},{12,140,268,396},{16,20..., dimensions={0} | all-to-all | bytes 9535488 | tf_op jit(solution)/shard_map/all_to_all | solution.py:232
  54.4 0.1 multiply_reduce_fusion.8
  54.4 1.1 fusion.2
  55.5 0.2 fusion.17
  55.8 0.4 pad_maximum_fusion
  56.1 13.4 %all_to_all.36 = f16[4,200,768]{2,1,0:T(8,128)(2,1)S(1)} all-to-all(f16[4,200,768]{2,1,0:T(8,128)(2,1)S(1)} %pad_maximum_fusion), channel_id=1, replica_groups={{0,4,8,12},{128,132,136,140},{256,260,264,268},{384,388,392,396},{16,14..., dimensions={0} | all-to-all | bytes 2457600 | tf_op jit(solution)/shard_map/all_to_all | solution.py:232
  69.6 0.0 copy-start.1
  69.6 0.0 copy-start.2
  69.6 0.0 copy-start.3
  69.7 0.2 fusion.5.tile_ref
  69.9 0.3 shard_map.88
  70.2 25.4 %all_to_all.37 = f16[16,80,128]{2,1,0:T(8,128)(2,1)S(1)} all-to-all(f16[16,80,128]{2,1,0:T(8,128)(2,1)S(1)} %convert_element_type.237), channel_id=1, replica_groups=mesh['x'=4,'zh'=4,'c'=2,'y'=4,'zl'=4] {'zh','zl'}, dimensions={0} | all-to-all | bytes 655360 | tf_op jit(solution)/shard_map/all_to_all | solution.py:23
  95.6 0.2 fusion.12
  95.8 0.1 multiply_reduce_fusion.grad_ref
  95.9 0.1 shard_map.89
  96.1 18.3 %all_to_all.38.part_ref = f32[32,1,128]{2,1,0:T(1,128)S(1)} all-to-all(f32[32,1,128]{2,1,0:T(1,128)S(1)} %shard_map.89), channel_id=1, replica_groups=mesh['x'=4,'zh'=4,'c'=2,'y'=4,'zl'=4] {'x','y','c'}, dimensions={0} | all-to-all | bytes 32768 | tf_op jit(solution)/shard_map/all_to_all | solution.py:23
  114.4 16.9 %all_to_all.39.square_ref = f32[16,1,128]{2,1,0:T(1,128)S(1)} all-to-all(f32[16,1,128]{2,1,0:T(1,128)S(1)} %shard_map.90), channel_id=1, replica_groups=mesh['x'=4,'zh'=4,'c'=2,'y'=4,'zl'=4] {'zh','zl'}, dimensions={0} | all-to-all | bytes 16384 | tf_op jit(solution)/shard_map/all_to_all | solution.py:23
  131.3 0.0 copy-done.1
  131.4 0.0 copy-done.2
  131.4 0.0 copy-done.3
  131.4 0.8 shard_map.91
  132.1 14.3 %all_to_all.40 = bf16[4,48,192]{2,1,0:T(8,128)(2,1)S(1)} all-to-all(bf16[4,48,192]{2,1,0:T(8,128)(2,1)S(1)} %get-tuple-element.15), channel_id=1, replica_groups=mesh['x'=4,'zh'=4,'c'=2,'y'=4,'zl'=4] {'zh'}, dimensions={0} | all-to-all | bytes 147456 | tf_op jit(solution)/shard_map/all_to_all | solution.py:23
  146.5 8.6 %all_to_all.41 = bf16[4,4,48,192]{3,2,1,0:T(8,128)(2,1)S(1)} all-to-all(bf16[4,4,48,192]{3,2,1,0:T(8,128)(2,1)S(1)} %broadcast_in_dim.9), channel_id=1, replica_groups=mesh['x'=4,'zh'=4,'c'=2,'y'=4,'zl'=4] {'x'}, dimensions={0} | all-to-all | bytes 589824 | tf_op jit(solution)/shard_map/all_to_all | solution.py:23
  155.1 7.2 %collective-permute-start.2 = (bf16[16,48,192]{2,1,0:T(8,128)(2,1)S(1)}, bf16[16,48,192]{2,1,0:T(8,128)(2,1)S(1)}, u32[]{:S(2)}, u32[]{:S(2)}) collective-permute-start(bf16[16,48,192]{2,1,0:T(8,128)(2,1)S(1)} %bitcast.64), channel_id=1, source_target_pairs={{0,16},{16,0},{1,17},{17,1},{2,18},{18,2},{3,19},{19,3},{4,20},{20... | collective-permute-start | bytes 884744 | tf_op jit(solution)/shard_map/ppermute | solution.py:19
  162.3 1.3 collective-permute-done.2
  163.6 0.2 maximum_select_fusion
  163.9 0.1 copy.12
  164.0 1.1 copy.13
  (7 shorter events, 0.2 us)
Async XLA Ops:
  0.6 17.5 %collective-permute-start.1 = (bf16[384,3072]{1,0:T(8,128)(2,1)}, bf16[384,3072]{1,0:T(8,128)(2,1)S(1)}, u32[]{:S(2)}, u32[]{:S(2)}) collective-permute-start(bf16[384,3072]{1,0:T(8,128)(2,1)} %acts_ref.1), channel_id=1, source_target_pairs={{0,16},{16,0},{1,17},{17,1},{2,18},{18,2},{3,19},{19,3},{4,20},{20... | collective-permute-start | bytes 7077896 | tf_op jit(solution)/shard_map/ppermute | solution.py:19
  9.4 8.1 %collective-permute-start = (bf16[384,1536]{1,0:T(8,128)(2,1)}, bf16[384,1536]{1,0:T(8,128)(2,1)S(1)}, u32[]{:S(2)}, u32[]{:S(2)}) collective-permute-start(bf16[384,1536]{1,0:T(8,128)(2,1)} %grads_ref.1), channel_id=1, source_target_pairs={{0,16},{16,0},{1,17},{17,1},{2,18},{18,2},{3,19},{19,3},{4,20},{20... | collective-permute-start | bytes 3538952 | tf_op jit(solution)/shard_map/ppermute | solution.py:19
  11.4 1.3 copy-start
  13.2 1.7 %copy-start.4 = (bf16[384,3072]{1,0:T(8,128)(2,1)S(1)}, bf16[384,3072]{1,0:T(8,128)(2,1)}, u32[]{:S(2)}) copy-start(bf16[384,3072]{1,0:T(8,128)(2,1)} %acts_ref.1) | copy-start | bytes 7077892
  69.6 61.7 %copy-start.1 = (f32[192,48]{0,1:T(8,128)S(1)}, f32[192,48]{0,1:T(8,128)}, u32[]{:S(2)}) copy-start(f32[192,48]{0,1:T(8,128)} %param.7) | copy-start | bytes 110596
  69.6 61.7 %copy-start.2 = (f32[192,48]{0,1:T(8,128)S(1)}, f32[192,48]{0,1:T(8,128)}, u32[]{:S(2)}) copy-start(f32[192,48]{0,1:T(8,128)} %param.8) | copy-start | bytes 110596
  69.6 61.7 %copy-start.3 = (f32[192,48]{0,1:T(8,128)S(1)}, f32[192,48]{0,1:T(8,128)}, u32[]{:S(2)}) copy-start(f32[192,48]{0,1:T(8,128)} %param.9) | copy-start | bytes 110596
  155.1 8.5 %collective-permute-start.2 = (bf16[16,48,192]{2,1,0:T(8,128)(2,1)S(1)}, bf16[16,48,192]{2,1,0:T(8,128)(2,1)S(1)}, u32[]{:S(2)}, u32[]{:S(2)}) collective-permute-start(bf16[16,48,192]{2,1,0:T(8,128)(2,1)S(1)} %bitcast.64), channel_id=1, source_target_pairs={{0,16},{16,0},{1,17},{17,1},{2,18},{18,2},{3,19},{19,3},{4,20},{20... | collective-permute-start | bytes 884744 | tf_op jit(solution)/shard_map/ppermute | solution.py:19
